TPU v7x, 32 devices: a whole 2x2x4 slice. The times are simulated.
32 devices in a mesh: dp: 16 (over z, y, x), patch: 2 (over core).
Axes of the slice: x: 2, y: 2, z: 4, core: 2. Of those that a mesh axis runs over, the one named last changes fastest.
Arguments:
- embedded_segments: bfloat16 [4608, 64, 128], P(('dp', 'patch')), may hold values from -6 to 6
- history_durations: int32 [4608], P(('dp', 'patch')), may hold values from 336 to 512, as said below
- segment_seen_indicator: int32 [4608, 64], P(('dp', 'patch')), may hold values from 0 to 1, as said below
- query_key_value_matrices: bfloat16 [2, 3, 128, 128], replicated, may hold values from -0.5 to 0.5
- mixing_result_matrices: bfloat16 [2, 128, 128], replicated, may hold values from -1.5 to 1.5
- first_dense_matrices: bfloat16 [2, 128, 256], replicated, may hold values from -0.5 to 0.5
- second_dense_matrices: bfloat16 [2, 256, 128], replicated, may hold values from -0.375 to 0.375
- batchnorm_scales: float32 [2, 2, 128], replicated, may hold values from 0.5 to 1.5
- batchnorm_offsets: float32 [2, 2, 128], replicated, may hold values from -3 to 3
- readout_matrix: bfloat16 [8192, 720], P('patch'), may hold values from -0.0625 to 0.0625
- prediction_cotangent: bfloat16 [4608, 720], P(('dp', 'patch')), may hold values from -6 to 6
Outputs:
- predictions: bfloat16 [4608, 720], P(('dp', 'patch'))
- input_grad: bfloat16 [4608, 64, 128], P(('dp', 'patch'))
- grad_attn_in: float32 [2, 3, 128, 128], replicated
- grad_attn_out: float32 [2, 128, 128], replicated
- grad_up: float32 [2, 128, 256], replicated
- grad_down: float32 [2, 256, 128], replicated
- grad_gain: float32 [2, 2, 128], replicated
- grad_shift: float32 [2, 2, 128], replicated
- grad_head: float32 [8192, 720], P('patch')
Inputs may be any that keep to these rules, and one draw needn't show every extreme that they name: `history_durations`: each is 336 or 512. `segment_seen_indicator`: the last patch of every series is observed.
All inputs are finite; a program needn't handle non-finite values.
Results may differ from a plain program's by a relative error of at most 0.028.
The roundings to bfloat16 on the way count: a program that leaves them out, or rounds other values in their place, can miss the bound.
Values may be sent and summed in bfloat16 or wider, within the bound.
A program may use at most 256 MiB of HBM per device.

v0:
```python
import math

import jax
import jax.numpy as jnp
from jax import lax
from jax.sharding import PartitionSpec as P

HEADS = 16
HEAD_DIM = 8


norm_eps = 1e-05
filler_score = -1e30


def project(left_side, right_side):
    return lax.dot_general(
        left_side,
        right_side,
        (((left_side.ndim - 1,), (0,)), ((), ())),
        preferred_element_type=jnp.float32,
    )


def project_back(left_side, right_side):
    return lax.dot_general(
        left_side,
        right_side,
        (((left_side.ndim - 1,), (1,)), ((), ())),
        preferred_element_type=jnp.float32,
    )


def outer_sum(left_side, right_side):
    left_rows = left_side.reshape(-1, left_side.shape[-1])
    right_rows = right_side.reshape(-1, right_side.shape[-1])
    return lax.dot_general(
        left_rows, right_rows, (((0,), (0,)), ((), ())), preferred_element_type=jnp.float32
    )


def series_blocks(function, arrays):
    series_count = arrays[0].shape[0]
    block_size = math.gcd(series_count, 16)
    stacked = tuple(
        (
            member.reshape((series_count // block_size, block_size) + member.shape[1:])
            for member in arrays
        )
    )
    result = lax.map(lambda block_items: function(*block_items), stacked)
    return jax.tree.map(lambda member: member.reshape((series_count,) + member.shape[2:]), result)


def masked_scores(query_heads, key_heads, valid_keys):
    scores = jnp.einsum(
        "bqhe,bkhe->bhqk", query_heads, key_heads, preferred_element_type=jnp.float32
    ) * HEAD_DIM ** (-0.5)
    return jnp.where(valid_keys[:, None, None, :] > 0.5, scores, filler_score)


def attend_forward(queries, key_rows, value_rows, valid_keys):
    series_count, query_count, model_width = queries.shape
    query_heads = queries.reshape(series_count, query_count, HEADS, HEAD_DIM)
    key_heads = key_rows.reshape(series_count, -1, HEADS, HEAD_DIM)
    value_heads = value_rows.reshape(series_count, -1, HEADS, HEAD_DIM)
    scores = masked_scores(query_heads, key_heads, valid_keys)
    top_score = jnp.max(scores, axis=-1, keepdims=True)
    exponential = jnp.exp(scores - top_score)
    total_weight = jnp.sum(exponential, axis=-1, keepdims=True)
    probabilities = (exponential / total_weight).astype(jnp.bfloat16)
    mixed_heads = jnp.einsum(
        "bhqk,bkhe->bqhe", probabilities, value_heads, preferred_element_type=jnp.float32
    )
    mixed_heads = mixed_heads.reshape(series_count, query_count, model_width).astype(jnp.bfloat16)
    return (mixed_heads, (top_score + jnp.log(total_weight))[..., 0])


def attend_backward(queries, key_rows, value_rows, valid_keys, log_total, grad_mixed):
    series_count, query_count, model_width = queries.shape
    query_heads = queries.reshape(series_count, query_count, HEADS, HEAD_DIM)
    key_heads = key_rows.reshape(series_count, -1, HEADS, HEAD_DIM)
    value_heads = value_rows.reshape(series_count, -1, HEADS, HEAD_DIM)
    grad_heads = grad_mixed.reshape(series_count, query_count, HEADS, HEAD_DIM)
    scores = masked_scores(query_heads, key_heads, valid_keys)
    probabilities = jnp.exp(scores - log_total[..., None])
    low_probability = probabilities.astype(jnp.bfloat16)
    grad_values = jnp.einsum(
        "bhqk,bqhe->bkhe", low_probability, grad_heads, preferred_element_type=jnp.float32
    )
    grad_weights = jnp.einsum(
        "bqhe,bkhe->bhqk", grad_heads, value_heads, preferred_element_type=jnp.float32
    )
    inner_sum = jnp.sum(probabilities * grad_weights, axis=-1, keepdims=True)
    grad_scores = (probabilities * (grad_weights - inner_sum)).astype(jnp.bfloat16)
    grad_queries = jnp.einsum(
        "bhqk,bkhe->bqhe", grad_scores, key_heads, preferred_element_type=jnp.float32
    ) * HEAD_DIM ** (-0.5)
    grad_keys = jnp.einsum(
        "bhqk,bqhe->bkhe", grad_scores, query_heads, preferred_element_type=jnp.float32
    ) * HEAD_DIM ** (-0.5)
    key_count = key_heads.shape[1]
    return (
        grad_queries.reshape(series_count, query_count, model_width),
        grad_keys.reshape(series_count, key_count, model_width),
        grad_values.reshape(series_count, key_count, model_width),
    )


def norm_forward(values, valid_own, gain_row, shift_row):
    weighted = valid_own[:, :, None]
    own_count = jnp.sum(valid_own)
    total_sums, valid_count = lax.psum(
        (jnp.sum(weighted * values, axis=(0, 1)), own_count), ("dp", "patch")
    )
    average = total_sums / valid_count
    centered = values - average
    variance = (
        lax.psum(jnp.sum(weighted * centered * centered, axis=(0, 1)), ("dp", "patch"))
        / valid_count
    )
    inverse_scale = lax.rsqrt(variance + norm_eps)
    normal_sample = centered * inverse_scale
    return (gain_row * normal_sample + shift_row, normal_sample, inverse_scale, valid_count)


def norm_backward(grad_output, normal_sample, inverse_scale, gain_row, valid_own, valid_count):
    weighted = valid_own[:, :, None]
    gain_grad, shift_grad = lax.psum(
        (
            jnp.sum(weighted * grad_output * normal_sample, axis=(0, 1)),
            jnp.sum(weighted * grad_output, axis=(0, 1)),
        ),
        ("dp", "patch"),
    )
    grad_input = (
        inverse_scale
        * gain_row
        * (grad_output - weighted * (shift_grad + normal_sample * gain_grad) / valid_count)
    )
    return (grad_input, gain_grad, shift_grad)


def per_device(
    embedded_segments,
    history_durations,
    segment_seen_indicator,
    query_key_value_matrices,
    mixing_result_matrices,
    first_dense_matrices,
    second_dense_matrices,
    batchnorm_scales,
    batchnorm_offsets,
    readout_matrix,
    prediction_cotangent,
):
    series_count, total_patches, model_width = embedded_segments.shape
    layer_total = query_key_value_matrices.shape[0]
    positions = jnp.arange(total_patches, dtype=jnp.int32)
    first_valid = total_patches - ((history_durations - 16) // 8 + 2)
    valid_own = (
        (positions[None, :] >= first_valid[:, None]) & (segment_seen_indicator > 0)
    ).astype(jnp.float32)
    hidden_state = embedded_segments.astype(jnp.float32)
    kept_state = []
    valid_count = jnp.float32(1.0)
    for layer_index in range(layer_total):
        weights_in = query_key_value_matrices[layer_index]
        rounded = hidden_state.astype(jnp.bfloat16)
        queries = project(rounded, weights_in[0]).astype(jnp.bfloat16)
        key_rows = project(rounded, weights_in[1]).astype(jnp.bfloat16)
        value_rows = project(rounded, weights_in[2]).astype(jnp.bfloat16)
        mixed_heads, log_total = series_blocks(
            attend_forward, (queries, key_rows, value_rows, valid_own)
        )
        attended = hidden_state + project(mixed_heads, mixing_result_matrices[layer_index])
        normed, normal_one, scale_one, valid_count = norm_forward(
            attended, valid_own, batchnorm_scales[layer_index, 0], batchnorm_offsets[layer_index, 0]
        )
        normed_low = normed.astype(jnp.bfloat16)
        hidden_units = project(normed_low, first_dense_matrices[layer_index]).astype(jnp.bfloat16)
        activated = jax.nn.gelu(hidden_units.astype(jnp.float32)).astype(jnp.bfloat16)
        summed = normed + project(activated, second_dense_matrices[layer_index])
        hidden_state, normal_two, scale_two, valid_count = norm_forward(
            summed, valid_own, batchnorm_scales[layer_index, 1], batchnorm_offsets[layer_index, 1]
        )
        kept_state.append(
            (
                rounded,
                queries,
                key_rows,
                value_rows,
                mixed_heads,
                log_total,
                normal_one,
                scale_one,
                normed_low,
                hidden_units,
                activated,
                normal_two,
                scale_two,
            )
        )
    flattened = (
        (hidden_state * valid_own[:, :, None]).astype(jnp.bfloat16).reshape(series_count, -1)
    )
    flat_mine = lax.all_to_all(flattened, "patch", split_axis=1, concat_axis=0, tiled=True)
    predictions = lax.psum_scatter(
        project(flat_mine, readout_matrix).astype(jnp.bfloat16),
        "patch",
        scatter_dimension=0,
        tiled=True,
    )
    complete_derivative = lax.all_gather(prediction_cotangent, "patch", axis=0, tiled=True)
    head_term = outer_sum(flat_mine, complete_derivative)
    grad_head = lax.psum(head_term, "dp")
    grad_rows = lax.all_to_all(
        project_back(complete_derivative, readout_matrix).astype(jnp.bfloat16),
        "patch",
        split_axis=0,
        concat_axis=1,
        tiled=True,
    ).astype(jnp.float32)
    grad_state = grad_rows.reshape(series_count, total_patches, model_width) * valid_own[:, :, None]
    grads_in, grads_out, grads_up, grads_down, gain_grads, shift_grads = ([], [], [], [], [], [])
    for layer_index in reversed(range(layer_total)):
        (
            rounded,
            queries,
            key_rows,
            value_rows,
            mixed_heads,
            log_total,
            normal_one,
            scale_one,
            normed_low,
            hidden_units,
            activated,
            normal_two,
            scale_two,
        ) = kept_state[layer_index]
        weights_in = query_key_value_matrices[layer_index]
        grad_summed, gain_two, shift_two = norm_backward(
            grad_state,
            normal_two,
            scale_two,
            batchnorm_scales[layer_index, 1],
            valid_own,
            valid_count,
        )
        grad_branch = grad_summed.astype(jnp.bfloat16)
        grads_down.append(outer_sum(activated, grad_branch))
        grad_active = project_back(grad_branch, second_dense_matrices[layer_index])
        unused_value, gelu_back = jax.vjp(jax.nn.gelu, hidden_units.astype(jnp.float32))
        grad_hidden = gelu_back(grad_active)[0].astype(jnp.bfloat16)
        grads_up.append(outer_sum(normed_low, grad_hidden))
        grad_normed = grad_summed + project_back(grad_hidden, first_dense_matrices[layer_index])
        grad_attended, gain_one, shift_one = norm_backward(
            grad_normed,
            normal_one,
            scale_one,
            batchnorm_scales[layer_index, 0],
            valid_own,
            valid_count,
        )
        gain_grads.append(jnp.stack([gain_one, gain_two]))
        shift_grads.append(jnp.stack([shift_one, shift_two]))
        grad_attn = grad_attended.astype(jnp.bfloat16)
        grads_out.append(outer_sum(mixed_heads, grad_attn))
        grad_mixed = project_back(grad_attn, mixing_result_matrices[layer_index]).astype(
            jnp.bfloat16
        )
        grad_queries, grad_keys, grad_values = series_blocks(
            attend_backward, (queries, key_rows, value_rows, valid_own, log_total, grad_mixed)
        )
        query_low = grad_queries.astype(jnp.bfloat16)
        key_low = grad_keys.astype(jnp.bfloat16)
        value_low = grad_values.astype(jnp.bfloat16)
        grads_in.append(
            jnp.stack(
                [
                    outer_sum(rounded, query_low),
                    outer_sum(rounded, key_low),
                    outer_sum(rounded, value_low),
                ]
            )
        )
        grad_state = (
            grad_attended
            + project_back(query_low, weights_in[0])
            + project_back(key_low, weights_in[1])
            + project_back(value_low, weights_in[2])
        )
    stacked_in = jnp.stack(grads_in[::-1])
    stacked_out = jnp.stack(grads_out[::-1])
    stacked_up = jnp.stack(grads_up[::-1])
    stacked_down = jnp.stack(grads_down[::-1])
    gain_stack = jnp.stack(gain_grads[::-1])
    shift_stack = jnp.stack(shift_grads[::-1])
    stacked_in, stacked_out, stacked_up, stacked_down = lax.psum(
        (stacked_in, stacked_out, stacked_up, stacked_down), ("dp", "patch")
    )
    input_grad = grad_state.astype(jnp.bfloat16)
    return (
        predictions,
        input_grad,
        stacked_in,
        stacked_out,
        stacked_up,
        stacked_down,
        gain_stack,
        shift_stack,
        grad_head,
    )


def solution(mesh):
    placed = (
        P(("dp", "patch"), None, None),
        P(("dp", "patch")),
        P(("dp", "patch"), None),
        P(),
        P(),
        P(),
        P(),
        P(),
        P(),
        P("patch", None),
        P(("dp", "patch"), None),
    )
    return jax.shard_map(
        per_device,
        mesh=mesh,
        in_specs=placed,
        out_specs=(
            P(("dp", "patch"), None),
            P(("dp", "patch"), None, None),
            P(),
            P(),
            P(),
            P(),
            P(),
            P(),
            P("patch", None),
        ),
        check_vma=False,
    )
```

profile of v0, /device:TPU:0, one launch (start us, length us, event | category | flops | bytes accessed | tf_op | source)
XLA Modules:
  0.0 1934.2 jit_solution(8529416427226255354)
XLA Ops:
  10.4 6.3 convolution_convert_fusion
  51.1 106.5 %while.52 = (s32[]{:T(128)}, bf16[9,16,64,128]{2,3,1,0:T(8,128)(2,1)}, f32[9,16,16,64]{3,2,1,0:T(8,128)}, bf16[9,16,64,128]{2,3,1,0:T(8,128)(2,1)}, f32[9,16,64]...) while((s32[]{:T(128)}, ...), condition=%wide.region_3.4_spmd, body=%wide.region_0.3_spmd.sunk | while | flops 46253056 | bytes 15280229 | solution.py:51
  163.3 42.5 %all-reduce.4 = (f32[128]{0:T(128)S(1)}, f32[]{:T(128)}) all-reduce(f32[128]{0:T(128)S(1)} %get-tuple-element.491, f32[]{:T(128)} %get-tuple-element.471), channel_id=1, replica_groups=mesh['dp'=16,'patch'=2] {'dp','patch'}, use_global_device_ids=true, to_apply=%region_5.6 | all-reduce | flops 129 | bytes 1032 | tf_op jit(solution)/shard_map/psum | solution.py:113
  210.2 40.4 %psum.165 = f32[128]{0:T(128)S(1)} all-reduce(f32[128]{0:T(128)S(1)} %fusion.126), channel_id=1, replica_groups=mesh['dp'=16,'patch'=2] {'dp','patch'}, use_global_device_ids=true, to_apply=%region_9.10 | all-reduce | flops 128 | bytes 1024 | tf_op jit(solution)/shard_map/psum | solution.py:119
  255.8 6.4 multiply_reduce_fusion.8
  262.2 39.9 %psum.166 = f32[128]{0:T(128)S(1)} all-reduce(f32[128]{0:T(128)S(1)} %get-tuple-element.493), channel_id=1, replica_groups=mesh['dp'=16,'patch'=2] {'dp','patch'}, use_global_device_ids=true, to_apply=%region_11.12 | all-reduce | flops 128 | bytes 1024 | tf_op jit(solution)/shard_map/psum | solution.py:113
  306.6 40.1 %psum.167 = f32[128]{0:T(128)S(1)} all-reduce(f32[128]{0:T(128)S(1)} %fusion.127), channel_id=1, replica_groups=mesh['dp'=16,'patch'=2] {'dp','patch'}, use_global_device_ids=true, to_apply=%region_13.14 | all-reduce | flops 128 | bytes 1024 | tf_op jit(solution)/shard_map/psum | solution.py:119
  364.2 7.4 reshape.350
  374.8 6.9 mul.491
  406.2 100.6 %while.53 = (s32[]{:T(128)}, bf16[9,16,64,128]{2,3,1,0:T(8,128)(2,1)}, f32[9,16,16,64]{3,2,1,0:T(8,128)S(1)}, bf16[9,16,64,128]{2,3,1,0:T(8,128)(2,1)}, f32[9,16...) while((s32[]{:T(128)}, ...), condition=%wide.region_17.18_spmd, body=%wide.region_14.17_spmd.sunk | while | flops 46253056 | bytes 15411301 | solution.py:51
  506.9 6.8 multiply_reduce_fusion.7
  513.7 40.0 %psum.168 = f32[128]{0:T(128)S(1)} all-reduce(f32[128]{0:T(128)S(1)} %get-tuple-element.495), channel_id=1, replica_groups=mesh['dp'=16,'patch'=2] {'dp','patch'}, use_global_device_ids=true, to_apply=%region_19.20 | all-reduce | flops 128 | bytes 1024 | tf_op jit(solution)/shard_map/psum | solution.py:113
  558.2 40.1 %psum.169 = f32[128]{0:T(128)S(1)} all-reduce(f32[128]{0:T(128)S(1)} %fusion.128), channel_id=1, replica_groups=mesh['dp'=16,'patch'=2] {'dp','patch'}, use_global_device_ids=true, to_apply=%region_21.22 | all-reduce | flops 128 | bytes 1024 | tf_op jit(solution)/shard_map/psum | solution.py:119
  602.9 6.4 multiply_reduce_fusion.6
  609.3 39.9 %psum.170 = f32[128]{0:T(128)S(1)} all-reduce(f32[128]{0:T(128)S(1)} %get-tuple-element.497), channel_id=1, replica_groups=mesh['dp'=16,'patch'=2] {'dp','patch'}, use_global_device_ids=true, to_apply=%region_23.24 | all-reduce | flops 128 | bytes 1024 | tf_op jit(solution)/shard_map/psum | solution.py:113
  653.6 40.1 %psum.171 = f32[128]{0:T(128)S(1)} all-reduce(f32[128]{0:T(128)S(1)} %fusion.129), channel_id=1, replica_groups=mesh['dp'=16,'patch'=2] {'dp','patch'}, use_global_device_ids=true, to_apply=%region_25.26 | all-reduce | flops 128 | bytes 1024 | tf_op jit(solution)/shard_map/psum | solution.py:119
  699.0 39.9 %all-reduce.3 = (f32[128]{0:T(128)S(1)}, f32[128]{0:T(128)S(1)}) all-reduce(f32[128]{0:T(128)S(1)} %multiply_reduce_fusion.5, f32[128]{0:T(128)S(1)} %reduce_sum.219), channel_id=1, replica_groups=mesh['dp'=16,'patch'=2] {'dp','patch'}, use_global_device_ids=true, to_apply=%region_31.32 | all-reduce | flops 256 | bytes 2048 | tf_op jit(solution)/shard_map/psum | solution.py:129
  738.9 9.1 subtract_multiply_fusion.3
  772.6 8.4 fusion.143
  781.0 8.5 fusion.110
  795.4 40.4 %all-reduce.2 = (f32[128]{0:T(128)S(1)}, f32[128]{0:T(128)S(1)}) all-reduce(f32[128]{0:T(128)S(1)} %get-tuple-element.380, f32[128]{0:T(128)S(1)} %get-tuple-element.379), channel_id=1, replica_groups=mesh['dp'=16,'patch'=2] {'dp','patch'}, use_global_device_ids=true, to_apply=%region_35.36 | all-reduce | flops 256 | bytes 2048 | tf_op jit(solution)/shard_map/psum | solution.py:129
  855.0 208.5 %while.54 = (s32[]{:T(128)}, bf16[9,16,64,128]{2,3,1,0:T(8,128)(2,1)}, bf16[9,16,64,128]{2,3,1,0:T(8,128)(2,1)}, bf16[9,16,64,128]{2,3,1,0:T(8,128)(2,1)}, bf16[...) while((s32[]{:T(128)}, ...), condition=%wide.region_38.39_spmd, body=%wide.region_36.38_spmd.sunk | while | flops 99861504 | bytes 39267464 | solution.py:51
  1079.4 9.4 multiply_reduce_fusion.11
  1088.8 40.1 %all-reduce.1 = (f32[128]{0:T(128)S(1)}, f32[128]{0:T(128)S(1)}) all-reduce(f32[128]{0:T(128)S(1)} %get-tuple-element.378, f32[128]{0:T(128)S(1)} %get-tuple-element.377), channel_id=1, replica_groups=mesh['dp'=16,'patch'=2] {'dp','patch'}, use_global_device_ids=true, to_apply=%region_42.43 | all-reduce | flops 256 | bytes 2048 | tf_op jit(solution)/shard_map/psum | solution.py:129
  1134.8 7.0 fusion.146
  1141.9 7.2 fusion.113
  1154.4 40.3 %all-reduce = (f32[128]{0:T(128)S(1)}, f32[128]{0:T(128)S(1)}) all-reduce(f32[128]{0:T(128)S(1)} %get-tuple-element.376, f32[128]{0:T(128)S(1)} %get-tuple-element.375), channel_id=1, replica_groups=mesh['dp'=16,'patch'=2] {'dp','patch'}, use_global_device_ids=true, to_apply=%region_46.47 | all-reduce | flops 256 | bytes 2048 | tf_op jit(solution)/shard_map/psum | solution.py:129
  1214.0 208.8 %while.55 = (s32[]{:T(128)}, bf16[9,16,64,128]{2,3,1,0:T(8,128)(2,1)}, bf16[9,16,64,128]{2,3,1,0:T(8,128)(2,1)}, bf16[9,16,64,128]{2,3,1,0:T(8,128)(2,1)}, bf16[...) while((s32[]{:T(128)}, ...), condition=%wide.region_49.50_spmd, body=%wide.region_47.49_spmd.sunk | while | flops 99861504 | bytes 39267464 | solution.py:51
  1441.4 8.3 fusion.219
  1464.6 101.9 %all-reduce.11.cloned.1.call-done = (f32[2,3,128,128]{2,3,1,0:T(8,128)}, f32[2,128,128]{2,1,0:T(8,128)}, f32[2,128,256]{2,1,0:T(8,128)}, f32[2,256,128]{2,1,0:T(8,128)}) async-done(((f32[2,3,128,128]{2,3,1,0:T(8,128)}, f32[2,128,128]{2,1,0:T(8,128)}, f32[2,128,256]{2,1,0:T(8,128)}, f32[2,256,128]{2,1,0:T(8,128)}), (f32[2,3,128,128]{2,3,1,0:T(8,128)}, f32[2,128,128]{2,1,0:T(8,128)}, ...) | async-done | bytes 1048592 | tf_op jit(solution)/shard_map/psum | solution.py:300
  1568.5 342.6 %all-reduce.9.cloned.1.call-done = f32[4096,720]{0,1:T(8,128)} async-done(((f32[4096,720]{0,1:T(8,128)}), f32[4096,720]{0,1:T(8,128)}) %all-reduce.9.cloned.1.call-update) | async-done | bytes 11796496 | tf_op jit(solution)/shard_map/psum | solution.py:216
  1916.0 10.3 copy.331
  (575 shorter events, 878.8 us)
Async XLA Ops:
  16.7 339.4 %all-to-all-start.1 = ((bf16[2,144,4096]{2,1,0:T(8,128)(2,1)}), bf16[2,144,4096]{2,1,0:T(8,128)(2,1)}, u32[]{:S(2)}, u32[]{:S(2)}) async-start(bf16[2,144,4096]{2,1,0:T(8,128)(2,1)} %bitcast.539), calls=%async_computation.2 | async-start | bytes 4718592 | tf_op jit(solution)/shard_map/all_to_all | solution.py:217
  28.8 226.9 %copy-start.42 = (f32[128]{0:T(128)}, f32[128]{0:T(128)S(1)}, u32[]{:S(2)}) copy-start(f32[128]{0:T(128)S(1)} %get-tuple-element.489) | copy-start | bytes 1540
  29.4 226.3 %copy-start.44 = (f32[128]{0:T(128)}, f32[128]{0:T(128)S(1)}, u32[]{:S(2)}) copy-start(f32[128]{0:T(128)S(1)} %get-tuple-element.485) | copy-start | bytes 1540
  51.1 106.5 %copy-start.25 = (bf16[2,128,128]{2,1,0:T(8,128)(2,1)S(1)}, bf16[2,128,128]{2,1,0:T(8,128)(2,1)}, u32[]{:S(2)}) copy-start(bf16[2,128,128]{2,1,0:T(8,128)(2,1)} %param.23) | copy-start | bytes 196612
  163.3 88.6 %copy-start.23 = (bf16[2,128,256]{2,1,0:T(8,128)(2,1)S(1)}, bf16[2,128,256]{2,1,0:T(8,128)(2,1)}, u32[]{:S(2)}) copy-start(bf16[2,128,256]{2,1,0:T(8,128)(2,1)} %param.24) | copy-start | bytes 393220
  206.3 49.4 %copy-start.35 = (f32[128]{0:T(128)}, f32[128]{0:T(128)S(1)}, u32[]{:S(2)}) copy-start(f32[128]{0:T(128)S(1)} %broadcast_divide_fusion.3) | copy-start | bytes 1540
  206.4 49.4 %slice-start = ((s8[4718592]{0:T(1024)(128)(4,1)}), s8[524288]{0:T(1024)(128)(4,1)S(1)}, s32[]{:S(2)}) async-start(s8[4718592]{0:T(1024)(128)(4,1)} %bitcast.468), calls=%async_computation.6 | async-start | bytes 1048576
  302.8 204.1 %copy-start.39 = (f32[128]{0:T(128)}, f32[128]{0:T(128)S(1)}, u32[]{:S(2)}) copy-start(f32[128]{0:T(128)S(1)} %broadcast_divide_fusion.2) | copy-start | bytes 1540
  347.8 159.1 %copy-start.37 = (f32[128]{0:T(128)}, f32[128]{0:T(128)S(1)}, u32[]{:S(2)}) copy-start(f32[128]{0:T(128)S(1)} %get-tuple-element.466) | copy-start | bytes 1540
  513.7 85.2 %copy-start.46 = (f32[128]{0:T(128)S(1)}, f32[128]{0:T(128)}, u32[]{:S(2)}) copy-start(f32[128]{0:T(128)} %get-tuple-element.490) | copy-start | bytes 1540
  513.7 85.2 %copy-start.47 = (f32[128]{0:T(128)S(1)}, f32[128]{0:T(128)}, u32[]{:S(2)}) copy-start(f32[128]{0:T(128)} %get-tuple-element.484) | copy-start | bytes 1540
  554.3 48.5 %slice-start.6 = ((s8[4718592]{0:T(1024)(128)(4,1)}), s8[524288]{0:T(1024)(128)(4,1)S(1)}, s32[]{:S(2)}) async-start(s8[4718592]{0:T(1024)(128)(4,1)} %bitcast.474), calls=%async_computation.12 | async-start | bytes 1048576
  694.4 44.5 %copy-start.62 = (f32[128]{0:T(128)S(1)}, f32[128]{0:T(128)}, u32[]{:S(2)}) copy-start(f32[128]{0:T(128)} %get-tuple-element.487) | copy-start | bytes 1540
  694.4 44.5 %copy-start.63 = (f32[128]{0:T(128)S(1)}, f32[128]{0:T(128)}, u32[]{:S(2)}) copy-start(f32[128]{0:T(128)} %get-tuple-element.483) | copy-start | bytes 1540
  738.9 9.1 copy-start.54
  738.9 9.1 copy-start.56
  755.6 679.5 %all-to-all-start = ((bf16[144,2,4096]{2,0,1:T(8,128)(2,1)}), bf16[144,2,4096]{2,0,1:T(8,128)(2,1)}, u32[]{:S(2)}, u32[]{:S(2)}) async-start(bf16[144,2,4096]{2,0,1:T(8,128)(2,1)} %copy.203), calls=%async_computation | async-start | bytes 4718592 | tf_op jit(solution)/shard_map/all_to_all | solution.py:207
  760.5 806.1 %all-reduce.11.cloned.1.call-start = ((), (), s32[]{:S(2)}) async-start(), calls=%async_computation.5 | async-start | bytes 2097152 | tf_op jit(solution)/shard_map/psum | solution.py:300
  766.7 14.2 slice-start.22
  772.6 16.9 slice-start.8
  781.0 8.6 slice-start.9
  835.7 243.1 %copy-start.58 = (f32[128]{0:T(128)}, f32[128]{0:T(128)S(1)}, u32[]{:S(2)}) copy-start(f32[128]{0:T(128)S(1)} %get-tuple-element.453) | copy-start | bytes 1540
  835.7 243.1 %copy-start.60 = (f32[128]{0:T(128)}, f32[128]{0:T(128)S(1)}, u32[]{:S(2)}) copy-start(f32[128]{0:T(128)S(1)} %get-tuple-element.454) | copy-start | bytes 1540
  855.0 208.5 %copy-start.3 = (bf16[144,64,128]{2,1,0:T(8,128)(2,1)S(1)}, bf16[144,64,128]{2,1,0:T(8,128)(2,1)}, u32[]{:S(2)}) copy-start(bf16[144,64,128]{2,1,0:T(8,128)(2,1)} %copy-done.2) | copy-start | bytes 7077892
  1067.8 9.2 slice-start.18
  1079.4 49.5 %copy-start.48 = (f32[128]{0:T(128)S(1)}, f32[128]{0:T(128)}, u32[]{:S(2)}) copy-start(f32[128]{0:T(128)} %get-tuple-element.465) | copy-start | bytes 1540
  1128.9 13.0 slice-start.24
  1134.8 14.3 slice-start.2
  1153.4 41.3 %copy-start.53 = (f32[128]{0:T(128)S(1)}, f32[128]{0:T(128)}, u32[]{:S(2)}) copy-start(f32[128]{0:T(128)} %get-tuple-element.463) | copy-start | bytes 1540
  1214.0 208.8 %copy-start.1 = (bf16[144,64,128]{2,1,0:T(8,128)(2,1)S(1)}, bf16[144,64,128]{2,1,0:T(8,128)(2,1)}, u32[]{:S(2)}) copy-start(bf16[144,64,128]{2,1,0:T(8,128)(2,1)} %param.19) | copy-start | bytes 7077892
  1435.0 133.5 %reduce-scatter.2.cloned.1.call-start = ((), (), s32[]{:S(2)}) async-start(), calls=%async_computation.3 | async-start | bytes 663552 | tf_op jit(solution)/shard_map/reduce_scatter | solution.py:208
  1441.3 469.7 %all-reduce.9.cloned.1.call-start = ((), (), s32[]{:S(2)}) async-start(), calls=%async_computation.4 | async-start | bytes 23592960 | tf_op jit(solution)/shard_map/psum | solution.py:216
  (67 other events, 305.3 us)
Sparse Core Ops, SparseCore 0:
  1435.1 131.3 all-reduce.10
  1573.6 337.4 all-reduce.8
Sparse Core Ops, SparseCore 1:
  1441.4 8.3 reduce-scatter.1
where the time goes:
time: 1950 us; the launch traced here: 1930 us
  matrix products  618 us (32%)
  blocking collectives  486 us (25%)
  waiting for transfers between devices  445 us (23%)
  other arithmetic  191 us (10%)
  local copies, waits for them, and re-layouts  166 us (9%)
    psum x1, waiting for transfers between devices, per_device(): grad_head = lax.psum(head_term, 'dp')  343 us
    psum x4, blocking collectives, norm_forward(): lax.psum((jnp.sum(weighted * values, axis=(0, 1)), own_count), ('dp', 'pa...  162 us
    psum x4, blocking collectives, norm_forward(): lax.psum(jnp.sum(weighted * centered * centered, axis=(0, 1)), ('dp', 'pa...  161 us
    psum x4, blocking collectives, norm_backward(): lax.psum((jnp.sum(weighted * grad_output * normal_sample, axis=(0, 1)), j...  161 us
    dot_general x36, matrix products, masked_scores(): jnp.einsum('bqhe,bkhe->bhqk', query_heads, key_heads, preferred_element_t...  121 us
    psum x1, waiting for transfers between devices, per_device(): lax.psum((stacked_in, stacked_out, stacked_up, stacked_down), ('dp', 'pat...  102 us
    dot_general x18, matrix products, attend_backward(): jnp.einsum('bqhe,bkhe->bhqk', grad_heads, value_heads, preferred_element_...  81.7 us
    dot_general x18, matrix products, attend_backward(): jnp.einsum('bhqk,bqhe->bkhe', grad_scores, query_heads, preferred_element...  74.4 us
  transfers between devices with their start and end apart: 5, of which 2 were waited for; matrix products, arithmetic and copies ran while one was open for 39% of the time, Pallas kernels for 0%

commit v1 on v0

v1 whole, which is shorter than its diff:
```python
import functools
import math

import jax
import jax.numpy as jnp
from jax import lax
from jax.experimental import pallas as pl
from jax.experimental.pallas import tpu as pltpu
from jax.sharding import PartitionSpec as P

HEADS = 16
HEAD_DIM = 8
WIDTH = 128
PATCHES = 64
PAIR = 2 * PATCHES
GROUPS = 4
GROUP_ROWS = WIDTH // GROUPS
GROUP_LANES = HEADS // GROUPS * PATCHES
SPREAD = HEADS * PATCHES
EPS = 1e-05
MASKED = -1e30
SCALE = HEAD_DIM**-0.5
SCALE_LOG2 = SCALE * math.log2(math.e)
GELU_IN = math.sqrt(2.0 / math.pi)
GELU_CUBE = 0.044715
CHUNK = 1024
READOUT_CHUNKS = 4
F32 = jnp.float32
BF16 = jnp.bfloat16
VMEM_BYTES = 60 * 2**20


def dot(left, right):
    return lax.dot_general(left, right, (((1,), (0,)), ((), ())), preferred_element_type=F32)


def dot_rows(left, right):
    return lax.dot_general(left, right, (((1,), (1,)), ((), ())), preferred_element_type=F32)


def turn(matrix):
    return matrix.astype(F32).T.astype(matrix.dtype)


def wide(column, lanes):
    return jnp.concatenate([column] * (lanes // WIDTH), axis=1)


def fold_lanes(values):
    total = values[:, :WIDTH]
    for start in range(WIDTH, values.shape[1], WIDTH):
        total = total + values[:, start : start + WIDTH]
    return total


def fold_heads(values):
    return jnp.concatenate([values] * (GROUP_LANES // WIDTH), axis=1)


def side_masks():
    lane = lax.broadcasted_iota(jnp.int32, (WIDTH, PAIR), 1)
    row = lax.broadcasted_iota(jnp.int32, (WIDTH, PAIR), 0)
    left = lane < PATCHES
    even = (row // HEAD_DIM) % 2 == 0
    return left, even


def token_mask(valid):
    return jnp.broadcast_to(valid, (WIDTH, valid.shape[1])).T


def shown_keys(keys, mask):
    parts = []
    for start in range(0, keys.shape[0], PATCHES):
        own = keys[start : start + PATCHES]
        parts.append(jnp.where(mask[start : start + PATCHES] > 0.5, own, own[PATCHES - 1 :]))
    return jnp.concatenate(parts, axis=0)


def spread_pair(tile, left, even, target):
    turned = pltpu.roll(tile, PATCHES, 1)
    keep = left == even
    first = jnp.where(keep, jnp.where(even, tile, turned), 0.0).astype(BF16)
    second = jnp.where(keep, jnp.where(even, turned, tile), 0.0).astype(BF16)
    step = 2 * HEAD_DIM
    for index in range(HEADS // 2):
        rows = slice(index * step, (index + 1) * step)
        lanes = slice(index * PAIR, (index + 1) * PAIR)
        target[0, rows, lanes] = first[rows]
        target[1, rows, lanes] = second[rows]


def halves(tile, left):
    return (
        jnp.where(left, tile, 0.0).astype(BF16),
        jnp.where(left, 0.0, tile).astype(BF16),
    )


def gather_heads(first, second, left):
    parts = []
    for head in range(HEADS // GROUPS):
        rows = slice(head * HEAD_DIM, (head + 1) * HEAD_DIM)
        lanes = slice(head // 2 * PAIR, (head // 2 + 1) * PAIR)
        one, two = first[rows, lanes], second[rows, lanes]
        if head % 2 == 0:
            two = pltpu.roll(two, PATCHES, 1)
        else:
            one = pltpu.roll(one, PATCHES, 1)
        parts.append(jnp.where(left[:HEAD_DIM], one, two))
    return jnp.concatenate(parts, axis=0)


def pair_lanes(pair):
    start = pair * PAIR
    return pl.ds(start if isinstance(start, int) else pl.multiple_of(start, PAIR), PAIR)


def pipeline(pairs, slots, score, soften, mix):
    even, odd = slots
    score(0, even)

    def two_pairs(index, carry):
        first = 2 * index
        mix(jnp.maximum(first - 1, 0), odd)
        score(first + 1, odd)
        soften(first, even)
        mix(first, even)
        score(jnp.minimum(first + 2, pairs - 1), even)
        soften(first + 1, odd)
        return carry

    lax.fori_loop(0, pairs // 2, two_pairs, 0, unroll=True)
    mix(pairs - 1, odd)


def chunks(lanes, work):
    for start in range(0, lanes, CHUNK):
        work(slice(start, start + CHUNK))


def device_at(index, sizes):
    return index // sizes[1], lax.rem(index, sizes[1])


def greet(step, sizes):
    others = sizes[0] * sizes[1]
    own = lax.axis_index("dp") * sizes[1] + lax.axis_index("patch")
    barrier = pltpu.get_barrier_semaphore()

    @pl.when(step == 0)
    def _():
        def signal(offset, carry):
            target = device_at(lax.rem(own + offset, others), sizes)
            pl.semaphore_signal(
                barrier, inc=1, device_id=target, device_id_type=pl.DeviceIdType.MESH
            )
            return carry

        lax.fori_loop(1, others, signal, 0)


def met(sizes):
    pl.semaphore_wait(pltpu.get_barrier_semaphore(), sizes[0] * sizes[1] - 1)


def second_step():
    return jnp.minimum(1, pl.num_programs(0) - 1)


def swap_tiles(sizes, tiles, send, arrive):
    others = sizes[0] * sizes[1]
    own = lax.axis_index("dp") * sizes[1] + lax.axis_index("patch")

    def start(offset, carry):
        pltpu.make_async_remote_copy(
            src_ref=tiles.at[own],
            dst_ref=tiles.at[own],
            send_sem=send,
            recv_sem=arrive,
            device_id=device_at(lax.rem(own + offset, others), sizes),
            device_id_type=pl.DeviceIdType.MESH,
        ).start()
        return carry

    lax.fori_loop(1, others, start, 0)
    await_bytes(tiles.at[pl.ds(0, others - 1)], arrive)
    await_bytes(tiles.at[pl.ds(0, others - 1)], send)


def await_bytes(like, sem):
    pltpu.make_async_copy(like, like, sem).wait()


def readout_copy(source, target, sems):
    return pltpu.make_async_remote_copy(
        src_ref=source,
        dst_ref=target,
        send_sem=sems.at[0],
        recv_sem=sems.at[1],
        device_id=(lax.axis_index("dp"), 1 - lax.axis_index("patch")),
        device_id_type=pl.DeviceIdType.MESH,
    )


def own_part(sizes, inner):
    chip = lax.axis_index("dp")
    return chip // inner, lax.rem(chip, inner) * sizes[1] + lax.axis_index("patch")


def first_patch(sizes, inner, patches, place):
    half = lax.rem(place + lax.axis_index("patch"), sizes[1])
    return (half * inner + place // sizes[1]) * (patches // (inner * sizes[1]))


class Spread:
    def __init__(self, sizes, inner, source, target, like, send, arrive):
        self.sizes, self.inner = sizes, inner
        self.source, self.target, self.like = source, target, like
        self.send, self.arrive = send, arrive
        self.devices = inner * sizes[1]
        self.group, self.own = own_part(sizes, inner)

    def start(self):
        def begin(offset, carry):
            other = lax.rem(self.own + offset, self.devices)
            pltpu.make_async_remote_copy(
                src_ref=self.source(other),
                dst_ref=self.target(self.own),
                send_sem=self.send,
                recv_sem=self.arrive,
                device_id=(
                    self.group * self.inner + other // self.sizes[1],
                    lax.rem(other, self.sizes[1]),
                ),
                device_id_type=pl.DeviceIdType.MESH,
            ).start()
            return carry

        pltpu.make_async_copy(
            self.source(self.own), self.target(self.own), self.arrive
        ).start()
        lax.fori_loop(1, self.devices, begin, 0)

    def receive(self):
        await_bytes(self.like(self.devices), self.arrive)

    def drain(self):
        await_bytes(self.like(self.devices - 1), self.send)

    def finish(self):
        self.receive()
        self.drain()


class Sharing:
    def __init__(self, sizes, inner, whole, source, slots, share, target, sems):
        rows = slots.shape[1]
        self.whole, self.source, self.slots, self.share = whole, source, slots, share

        def part(ref, place):
            return ref.at[pl.ds(pl.multiple_of(place * rows, rows), rows)]

        self.stages = [
            Spread(
                sizes,
                inner,
                lambda place: part(source, place),
                lambda place: slots.at[place],
                lambda count: slots.at[pl.ds(0, count)],
                sems.at[0, 0],
                sems.at[0, 1],
            ),
            Spread(
                sizes,
                inner,
                lambda place: share,
                lambda place: part(target, place),
                lambda count: target.at[pl.ds(0, rows * count)],
                sems.at[1, 0],
                sems.at[1, 1],
            ),
        ]

    def begin(self):
        self.source[...] = self.whole[...].astype(self.source.dtype)
        self.stages[0].start()

    def add(self):
        total = self.slots[0].astype(F32)
        for place in range(1, self.slots.shape[0]):
            total = total + self.slots[place].astype(F32)
        self.share[...] = total.astype(self.share.dtype)


def sharing_dtype(devices):
    return BF16 if 4 * WIDTH // devices % 16 == 0 else F32


def sharing_scratch(devices):
    rows = 4 * WIDTH // devices
    dtype = sharing_dtype(devices)
    return [
        pltpu.VMEM((4 * WIDTH, WIDTH), dtype),
        pltpu.VMEM((devices, rows, WIDTH), dtype),
        pltpu.VMEM((rows, WIDTH), dtype),
        pltpu.SemaphoreType.DMA((2, 2)),
    ]


def ship_rows(sizes, inner, flat, start, slots, send, arrive):
    patches = flat.shape[0]
    part, count = slots.shape[1:3]
    return Spread(
        sizes,
        inner,
        lambda place: flat.at[
            pl.ds(first_patch(sizes, inner, patches, place), part), pl.ds(start, count)
        ],
        lambda slot: slots.at[slot],
        lambda places: slots.at[pl.ds(0, places)],
        send,
        arrive,
    )


def as_columns(row):
    return jnp.broadcast_to(row, (WIDTH, WIDTH)).T


def norm_stats(step, sizes, values, valid, gains, out, scratch):
    pivot, sums, squares, count, tiles, send, arrive = scratch
    lanes = valid.shape[-1]

    @pl.when(step == 0)
    def _():
        own = jnp.sum(valid[...])
        first = jnp.sum(fold_lanes(values[...] * valid[...]), axis=1, keepdims=True) / own
        pivot[...] = jnp.broadcast_to(first, (WIDTH, WIDTH))
        sums[...] = jnp.zeros_like(sums)
        squares[...] = jnp.zeros_like(squares)
        count[...] = jnp.zeros_like(count)

    def add(at):
        centred = (values[:, at] - wide(pivot[...], CHUNK)) * valid[:, at]
        sums[...] += fold_lanes(centred)
        squares[...] += fold_lanes(centred * centred)
        count[...] += jnp.broadcast_to(fold_lanes(valid[:, at]), count.shape)

    chunks(lanes, add)

    @pl.when(step == pl.num_programs(0) - 1)
    def _():
        own = lax.axis_index("dp") * sizes[1] + lax.axis_index("patch")
        total = jnp.broadcast_to(jnp.sum(count[0:1, :]), (1, WIDTH))
        shift = jnp.sum(sums[...].T, axis=0, keepdims=True)
        square = jnp.sum(squares[...].T, axis=0, keepdims=True)
        tiles[own, 0:1, :] = pivot[...].T[0:1, :] + shift / total
        tiles[own, 1:2, :] = square - shift * shift / total
        tiles[own, 2:3, :] = total
        tiles[own, 3:8, :] = jnp.zeros((5, WIDTH), F32)
        swap_tiles(sizes, tiles, send, arrive)
        means, spreads, counts = tiles[:, 0, :], tiles[:, 1, :], tiles[:, 2, :]
        total = jnp.sum(counts, axis=0, keepdims=True)
        mean = jnp.sum(means * counts, axis=0, keepdims=True) / total
        apart = means - mean
        variance = jnp.sum(spreads + counts * (apart * apart), axis=0, keepdims=True) / total
        inverse = lax.rsqrt(variance + EPS)
        out[0] = as_columns(mean)
        out[1] = as_columns(inverse)
        out[2] = as_columns(inverse * gains[0])
        out[3] = as_columns(gains[1])
        out[4] = as_columns(total)
        out[5] = as_columns(gains[0])


def add_gradient(grad, normal, valid, scratch):
    weighted = grad * valid
    scratch[0][...] += fold_lanes(weighted * normal)
    scratch[1][...] += fold_lanes(weighted)


def clear_gradient(step, scratch):
    @pl.when(step == 0)
    def _():
        scratch[0][...] = jnp.zeros_like(scratch[0])
        scratch[1][...] = jnp.zeros_like(scratch[1])


def gradient_sums(step, sizes, columns, columns_out, rows_out, scratch):
    by_normal, plain, tiles, send, arrive = scratch

    @pl.when(step == pl.num_programs(0) - 1)
    def _():
        own = lax.axis_index("dp") * sizes[1] + lax.axis_index("patch")
        tiles[own, 0:1, :] = jnp.sum(by_normal[...].T, axis=0, keepdims=True)
        tiles[own, 1:2, :] = jnp.sum(plain[...].T, axis=0, keepdims=True)
        tiles[own, 2:8, :] = jnp.zeros((6, WIDTH), F32)
        swap_tiles(sizes, tiles, send, arrive)
        summed = jnp.sum(tiles[...], axis=0)
        rows_out[...] = summed
        total = columns[4]
        columns_out[0] = as_columns(summed[0:1, :]) / total
        columns_out[1] = as_columns(summed[1:2, :]) / total


def apply_norm(values, columns):
    lanes = values.shape[1]
    return (values - wide(columns[0], lanes)) * wide(columns[2], lanes) + wide(columns[3], lanes)


def normalise(values, columns):
    lanes = values.shape[1]
    return (values - wide(columns[0], lanes)) * wide(columns[1], lanes)


def back_norm(grad, normal, valid, columns, back_columns):
    lanes = grad.shape[1]
    inner = wide(back_columns[1], lanes) + normal * wide(back_columns[0], lanes)
    return wide(columns[2], lanes) * (grad - valid * inner)


def attention_forward_body(sizes, layer, first_layer, makes_head, *refs):
    if first_layer:
        x_ref, readout, refs = refs[0], refs[1], refs[2:]
        columns = None
    else:
        x_ref, columns, refs = refs[0], refs[1], refs[2:]
    w_in_ref, w_out_ref, valid_ref, scales, offsets = refs[:5]
    refs = refs[5:]
    if makes_head:
        head_refs, refs = refs[:3], refs[3:]
    h_out, qkv_out, o_out, lse_out, columns_out = refs[:5]
    refs = refs[5:]
    if first_layer:
        readout_out, readout_sems = refs[0], refs[-1]
        refs = refs[1:-1]
    if makes_head:
        head_refs, refs = head_refs + refs[:1], refs[1:]
    size = len(FORWARD_SLOT)
    slots, refs = (refs[:size], refs[size : 2 * size]), refs[2 * size :]
    (x_full, q_full, k_rows, tops, sums, w_in, w_out), scratch = refs[:7], refs[7:]
    step = pl.program_id(0)
    greet(step, sizes)

    @pl.when(step == second_step())
    def _():
        met(sizes)
        if first_layer:
            readout_copy(readout, readout_out, readout_sems).start()

    lanes = h_out.shape[-1]
    pairs = lanes // PAIR

    @pl.when(step == 0)
    def _():
        for slot in slots:
            slot[0][...] = jnp.zeros_like(slot[0])
        for part in range(3):
            w_in[part * WIDTH : (part + 1) * WIDTH, :] = turn(w_in_ref[0, part])
        w_out[...] = turn(w_out_ref[0])

    if makes_head:
        head_backward(step, *head_refs)

    def project(at):
        x = x_ref[at, :].astype(F32).T if first_layer else apply_norm(x_ref[0, :, at], columns)
        x_full[:, at] = x
        low = x.astype(BF16)
        q = dot(w_in[0:WIDTH, :], low)
        q_full[:, at] = q
        qkv_out[0, 0:WIDTH, at] = q.astype(BF16)
        k = dot(w_in[WIDTH : 2 * WIDTH, :], low)
        k_rows[at, :] = shown_keys(k.T, token_mask(valid_ref[0, :, at])).astype(BF16)
        qkv_out[0, WIDTH : 2 * WIDTH, at] = k.astype(BF16)
        qkv_out[0, 2 * WIDTH :, at] = dot(w_in[2 * WIDTH :, :], low).astype(BF16)

    chunks(lanes, project)
    left, even = side_masks()

    def score(pair, slot):
        spread, scores, _ = slot
        at = pair_lanes(pair)
        spread_pair(q_full[:, at], left, even, spread)
        keys = k_rows[at, :]
        for side in range(2):
            own = slice(side * PATCHES, (side + 1) * PATCHES)
            for group in range(GROUPS):
                cut = slice(group * GROUP_LANES, (group + 1) * GROUP_LANES)
                scores[own, cut] = dot(keys[own], spread[side, :, cut])

    def soften(pair, slot):
        _, scores, weights = slot
        for side in range(2):
            own = slice(side * PATCHES, (side + 1) * PATCHES)
            for group in range(GROUPS):
                cut = slice(group * GROUP_LANES, (group + 1) * GROUP_LANES)
                shown = scores[own, cut]
                top = jnp.max(shown, axis=0, keepdims=True)
                weights[own, cut] = jnp.exp2((shown - top) * SCALE_LOG2).astype(BF16)
                tops[pl.ds(2 * pair + side, 1), cut] = top

    def mix(pair, slot):
        _, _, weights = slot
        at = pair_lanes(pair)
        valid = valid_ref[0, :, at]
        v_one, v_two = halves(qkv_out[0, 2 * WIDTH :, at].astype(F32) * valid, left)
        ones = jnp.broadcast_to(valid, (HEAD_DIM, PAIR))
        some = left[:HEAD_DIM]
        ones = jnp.concatenate([jnp.where(some, ones, 0.0), jnp.where(some, 0.0, ones)], axis=0)
        ones = ones.astype(BF16)
        for group in range(GROUPS):
            cut = slice(group * GROUP_LANES, (group + 1) * GROUP_LANES)
            rows = slice(group * GROUP_ROWS, (group + 1) * GROUP_ROWS)
            mixed = dot(
                jnp.concatenate([v_one[rows], v_two[rows], ones], axis=0), weights[:, cut]
            )
            products = []
            for side in range(2):
                start = 2 * GROUP_ROWS + side * HEAD_DIM
                total = mixed[start : start + HEAD_DIM]
                sums[pl.ds(2 * pair + side, 1), cut] = total[0:1]
                inverse = jnp.concatenate([1.0 / total] * (GROUP_ROWS // HEAD_DIM), axis=0)
                products.append(mixed[side * GROUP_ROWS : (side + 1) * GROUP_ROWS] * inverse)
            o_out[0, rows, at] = gather_heads(*products, left).astype(BF16)

    pipeline(pairs, slots, score, soften, mix)
    lse_out[0] = tops[...] * SCALE_LOG2 + jnp.log2(sums[...])

    def attend(at):
        h_out[0, :, at] = x_full[:, at] + dot(w_out[...], o_out[0, :, at])

    chunks(lanes, attend)
    if first_layer:

        @pl.when(step == pl.num_programs(0) - 1)
        def _():
            readout_copy(readout, readout_out, readout_sems).wait()

    gains = scales[layer, 0:1, :], offsets[layer, 0:1, :]
    norm_stats(step, sizes, h_out.at[0], valid_ref.at[0], gains, columns_out, scratch)


def feed_forward_body(
    sizes, layer, h_ref, columns, w_up_ref, w_down_ref, valid_ref, scales, offsets,
    f_out, columns_out, w_up, w_down, *scratch,
):
    step = pl.program_id(0)
    greet(step, sizes)

    @pl.when(step == second_step())
    def _():
        met(sizes)

    @pl.when(step == 0)
    def _():
        w_up[...] = turn(w_up_ref[0])
        w_down[...] = turn(w_down_ref[0])

    def feed(at):
        normed = apply_norm(h_ref[0, :, at], columns)
        low = normed.astype(BF16)
        active = []
        for start in range(0, w_up.shape[0], WIDTH):
            u = dot(w_up[start : start + WIDTH, :], low).astype(BF16).astype(F32)
            bent = jnp.tanh(u * (GELU_IN + (GELU_IN * GELU_CUBE) * (u * u)))
            half = 0.5 * u
            active.append((half + half * bent).astype(BF16))
        f_out[0, :, at] = normed + dot(w_down[...], jnp.concatenate(active, axis=0))

    chunks(h_ref.shape[-1], feed)
    gains = scales[layer, 1:2, :], offsets[layer, 1:2, :]
    norm_stats(step, sizes, f_out.at[0], valid_ref.at[0], gains, columns_out, scratch)


def turn_body(
    sizes, f_ref, columns, valid_ref, gz_ref, flat_out, gx_out, back_out, rows_out, turned,
    *scratch,
):
    step = pl.program_id(0)
    patches, block = gz_ref.shape[:2]
    greet(step, sizes)

    @pl.when(step == second_step())
    def _():
        met(sizes)

    clear_gradient(step, scratch)
    shift = lax.axis_index("patch") * (patches // sizes[1])

    def rows_at(patch):
        return pl.ds(lax.rem(patch + shift, patches), block, stride=patches)

    def show(at):
        turned[at, :] = (apply_norm(f_ref[0, :, at], columns) * valid_ref[0, :, at]).T

    def take(at):
        valid = valid_ref[0, :, at]
        grad = turned[at, :].T * valid
        gx_out[0, :, at] = grad
        add_gradient(grad, normalise(f_ref[0, :, at], columns), valid, scratch)

    chunks(f_ref.shape[-1], show)
    for patch in range(patches):
        flat_out[patch] = turned[rows_at(patch), :].astype(BF16)
    for patch in range(patches):
        turned[rows_at(patch), :] = gz_ref[patch]
    chunks(f_ref.shape[-1], take)

    gradient_sums(step, sizes, columns, back_out, rows_out, scratch)


def head_backward(step, cotangent, readout_own, readout_other, out):
    def rows(readout):
        grad = dot(cotangent[...], readout[...])
        for patch in range(out.shape[0]):
            out[patch] = grad[:, patch * WIDTH : (patch + 1) * WIDTH]

    pl.when(step < READOUT_CHUNKS)(lambda: rows(readout_own))
    pl.when((step >= READOUT_CHUNKS) & (step < 2 * READOUT_CHUNKS))(lambda: rows(readout_other))


def head_forward(step, flat, readout_own, readout_other, out, total):
    @pl.when(step == 0)
    def _():
        total[...] = jnp.zeros_like(total)

    def rows(readout):
        for patch in range(0, flat.shape[0], 2):
            pair = jnp.concatenate([flat[patch], flat[patch + 1]], axis=1)
            total[...] += dot_rows(pair, readout[:, patch * WIDTH : (patch + 2) * WIDTH])

    pl.when(step < READOUT_CHUNKS)(lambda: rows(readout_own))
    pl.when((step >= READOUT_CHUNKS) & (step < 2 * READOUT_CHUNKS))(lambda: rows(readout_other))

    @pl.when(step == 2 * READOUT_CHUNKS - 1)
    def _():
        out[...] = total[...].astype(out.dtype)


def head_specs(horizon, half_rows, patches, series):
    chunk = half_rows // READOUT_CHUNKS
    last = 2 * READOUT_CHUNKS - 1
    flat_spec = pl.BlockSpec(
        (chunk // WIDTH, series, WIDTH), lambda step: (jnp.minimum(step, last), 0, 0)
    )
    own_spec = pl.BlockSpec(
        (horizon, chunk), lambda step: (0, jnp.minimum(step, READOUT_CHUNKS - 1))
    )
    other_spec = pl.BlockSpec(
        (horizon, chunk),
        lambda step: (0, jnp.clip(step - READOUT_CHUNKS, 0, READOUT_CHUNKS - 1)),
    )
    return flat_spec, own_spec, other_spec


def head_gradient_body(*refs):
    *parts, cotangent, out, total = refs
    step = pl.program_id(0)

    @pl.when(step == 0)
    def _():
        total[...] = jnp.zeros_like(total)

    sources, part, _, width = parts[0].shape
    start = 0
    for rows in parts:
        count = rows.shape[2]
        right = cotangent[:, start : start + count].reshape(sources * count, -1)
        start += count
        for patch in range(part):
            left = rows[:, patch].reshape(sources * count, width)
            total[patch] += lax.dot_general(
                left, right, (((0,), (0,)), ((), ())), preferred_element_type=F32
            )

    @pl.when(step == pl.num_programs(0) - 1)
    def _():
        for patch in range(part):
            out[:, patch * width : (patch + 1) * width] = total[patch].T.astype(out.dtype)


def widen_body(layers, *refs):
    rows, summed, *tiles = refs[: 2 + 2 * layers]
    out, in_out, out_out, up_out, down_out, gain_out, shift_out = refs[2 + 2 * layers :]
    for at in range(rows.shape[0]):
        width = rows.shape[-1]
        out[:, at * width : (at + 1) * width] = rows[at].astype(out.dtype)

    @pl.when(pl.program_id(0) == 0)
    def _():
        for layer in range(layers):
            attention = 2 * (layers - layer) if layer else 0
            feed = 2 * (layers - layer) - 1
            out_out[layer] = summed[attention, 0:WIDTH, :].astype(F32)
            for part in range(3):
                rows_of_part = slice((part + 1) * WIDTH, (part + 2) * WIDTH)
                in_out[layer, part] = summed[attention, rows_of_part, :].astype(F32)
            up_out[layer, :, :WIDTH] = summed[feed, :WIDTH, :].astype(F32)
            up_out[layer, :, WIDTH:] = summed[feed, WIDTH : 2 * WIDTH, :].astype(F32)
            down_out[layer] = summed[feed, 2 * WIDTH :, :].astype(F32)
            for norm in range(2):
                tile = tiles[2 * layer + norm]
                gain_out[layer, norm : norm + 1, :] = tile[0:1, :]
                shift_out[layer, norm : norm + 1, :] = tile[1:2, :]


def feed_backward_body(sizes, inner, ships, *refs):
    (gx_ref, f_ref, h_ref, columns_two, back_two, columns_one, w_down, w_up,
     valid_ref), refs = refs[:9], refs[9:]
    if ships:
        flat_chunk, readout_own, readout_other, flat, *refs = refs
        gy_out, weights_out, back_out, rows_out, out, slots_out, total, *scratch = refs
        scratch, row_sems = scratch[:-1], scratch[-1]
        rows_sent = ship_rows(sizes, inner, flat, 0, slots_out, row_sems.at[0], row_sems.at[1])
    else:
        gy_out, weights_out, back_out, rows_out, *scratch = refs
    step = pl.program_id(0)
    greet(step, sizes)

    @pl.when(step == second_step())
    def _():
        met(sizes)
        if ships:
            rows_sent.start()

    if ships:
        head_forward(step, flat_chunk, readout_own, readout_other, out, total)
    active_full, low_full, normed_full, units_full, w_up_turned, *scratch = scratch
    clear_gradient(step, scratch)

    @pl.when(step == 0)
    def _():
        weights_out[...] = jnp.zeros_like(weights_out)
        w_up_turned[...] = turn(w_up[0])

    def feed(at):
        valid = valid_ref[0, :, at]
        normed = apply_norm(h_ref[0, :, at], columns_one).astype(BF16)
        normed_full[:, at] = normed
        normal = normalise(f_ref[0, :, at], columns_two)
        grad = back_norm(gx_ref[0, :, at], normal, valid, columns_two, back_two)
        low = grad.astype(BF16)
        low_full[:, at] = low
        grad_units = []
        for start in range(0, w_down.shape[1], WIDTH):
            rows = slice(start, start + WIDTH)
            u = dot(w_up_turned[rows, :], normed).astype(BF16).astype(F32)
            square = u * u
            bent = jnp.tanh(u * (GELU_IN + (GELU_IN * GELU_CUBE) * square))
            half = 0.5 + 0.5 * bent
            active_full[rows, at] = (u * half).astype(BF16)
            inner = (0.5 * GELU_IN) + (1.5 * GELU_IN * GELU_CUBE) * square
            slope = half + (u * inner) * (1.0 - bent * bent)
            grad_units.append((dot(w_down[0, rows, :], low) * slope).astype(BF16))
            units_full[rows, at] = grad_units[-1]
        normal = normalise(h_ref[0, :, at], columns_one)
        grad_normed = grad + dot(w_up[0], jnp.concatenate(grad_units, axis=0))
        gy_out[0, :, at] = grad_normed
        add_gradient(grad_normed, normal, valid, scratch)

    chunks(gx_ref.shape[-1], feed)
    weights_out[2 * WIDTH :, :] += dot_rows(active_full[...], low_full[...])
    by_up = dot_rows(normed_full[...], units_full[...])
    weights_out[0:WIDTH, :] += by_up[:, :WIDTH]
    weights_out[WIDTH : 2 * WIDTH, :] += by_up[:, WIDTH:]
    if ships:
        pl.when(step == pl.num_programs(0) - 1)(rows_sent.finish)
    gradient_sums(step, sizes, columns_one, back_out, rows_out, scratch)


def attention_backward_body(sizes, inner, first_layer, opens, closes, start, *refs):
    (gy_ref, h_ref, qkv_ref, o_ref, lse_ref, valid_ref, columns_one, back_one, w_out, w_in_ref,
     x_ref), refs = refs[:11], refs[11:]
    taken = made = None
    if first_layer:
        ready, (gx_out, summed_out), refs = refs[:3], refs[3:5], refs[5:]
        arrays = 1 + len(ready)
        each = len(sharing_scratch(inner * sizes[1]))
        refs, weights_out, shared = (
            refs[: -1 - each * arrays],
            refs[-1 - each * arrays],
            refs[-each * arrays :],
        )
        shares = []
        for at, whole in enumerate((weights_out,) + tuple(ready)):
            source, slots, share, sems = shared[each * at : each * (at + 1)]
            shares.append(
                Sharing(sizes, inner, whole, source, slots, share, summed_out.at[at], sems)
            )
    else:
        columns_prev, *refs = refs
        if start:
            flat, *refs = refs
        if not opens:
            _, taken, *refs = refs
            taken, made = (taken, refs[0]), None
            refs = refs[1:]
        if closes:
            gx_out, weights_out, back_out, rows_out, *refs = refs
        else:
            gx_out, weights_out, made, *refs = refs
        if start:
            slots_out, *refs, row_sems = refs
            rows_sent = ship_rows(
                sizes, inner, flat, start, slots_out, row_sems.at[0], row_sems.at[1]
            )
        count = len(SUM_SCRATCH) + len(swap_scratch(sizes))
        refs, scratch = refs[:-count], refs[-count:]
    size = len(BACKWARD_SLOT)
    slots = refs[:size], refs[size : 2 * size]
    low_full, grad_full, g_full, k_rows, v_rows, grads, w_in = refs[2 * size :]
    step = pl.program_id(0)
    last = pl.num_programs(0) - 1
    if closes or start:
        greet(step, sizes)

        @pl.when(step == second_step())
        def _():
            met(sizes)
            if first_layer:
                for share in shares[1:]:
                    share.begin()
            elif start:
                rows_sent.start()

    if first_layer:

        @pl.when(step == jnp.maximum(second_step(), last // 2 + 1))
        def _():
            for share in shares[1:]:
                share.stages[0].receive()
                share.add()
                share.stages[1].start()

    lanes = valid_ref.shape[-1]
    pairs = lanes // PAIR

    @pl.when(step == 0)
    def _():
        for slot in slots:
            slot[0][...] = jnp.zeros_like(slot[0])
            slot[1][...] = jnp.zeros_like(slot[1])
        weights_out[...] = jnp.zeros_like(weights_out) if taken is None else taken[0][...]
        for part in range(3):
            w_in[:, part * WIDTH : (part + 1) * WIDTH] = w_in_ref[0, part]

    if not first_layer and taken is None:
        clear_gradient(step, scratch)
    elif not first_layer:

        @pl.when(step == 0)
        def _():
            scratch[0][...] = taken[1][0]
            scratch[1][...] = taken[1][1]

    def prepare(at):
        normal = normalise(h_ref[0, :, at], columns_one)
        grad = back_norm(gy_ref[0, :, at], normal, valid_ref[0, :, at], columns_one, back_one)
        grad_full[:, at] = grad
        low = grad.astype(BF16)
        low_full[:, at] = low
        g_full[:, at] = dot(w_out[0], low).astype(BF16).astype(F32)
        mask = token_mask(valid_ref[0, :, at])
        keys = shown_keys(qkv_ref[0, WIDTH : 2 * WIDTH, at].astype(F32).T, mask)
        k_rows[at, :] = keys.astype(BF16)
        v_rows[at, :] = (qkv_ref[0, 2 * WIDTH :, at].astype(F32).T * mask).astype(BF16)

    chunks(lanes, prepare)
    weights_out[0:WIDTH, :] += dot_rows(o_ref[0], low_full[...])
    left, even = side_masks()

    def score(pair, slot):
        spread_q, spread_g, scores, pulls, _, _, inner = slot
        at = pair_lanes(pair)
        spread_pair(qkv_ref[0, 0:WIDTH, at].astype(F32), left, even, spread_q)
        grad = g_full[:, at]
        spread_pair(grad, left, even, spread_g)
        keys = k_rows[at, :]
        content = v_rows[at, :]
        for side in range(2):
            own = slice(side * PATCHES, (side + 1) * PATCHES)
            for group in range(GROUPS):
                cut = slice(group * GROUP_LANES, (group + 1) * GROUP_LANES)
                scores[own, cut] = dot(keys[own], spread_q[side, :, cut])
                pulls[own, cut] = dot(content[own], spread_g[side, :, cut])
        products = grad * o_ref[0, :, at].astype(F32)
        some = left[:HEAD_DIM]
        for head in range(0, HEADS, 2):
            both = [
                jnp.broadcast_to(
                    jnp.sum(products[start : start + HEAD_DIM], axis=0, keepdims=True),
                    (HEAD_DIM, PAIR),
                )
                for start in (head * HEAD_DIM, (head + 1) * HEAD_DIM)
            ]
            turned = [pltpu.roll(row, PATCHES, 1) for row in both]
            lanes_of = slice(head * PATCHES, (head + 2) * PATCHES)
            inner[0, :, lanes_of] = jnp.where(some, both[0], turned[1])
            inner[1, :, lanes_of] = jnp.where(some, turned[0], both[1])

    def soften(pair, slot):
        _, _, scores, pulls, weights, slopes, inner = slot
        for side in range(2):
            own = slice(side * PATCHES, (side + 1) * PATCHES)
            for group in range(GROUPS):
                cut = slice(group * GROUP_LANES, (group + 1) * GROUP_LANES)
                total = lse_ref[0, pl.ds(2 * pair + side, 1), cut]
                weight = jnp.exp2(scores[own, cut] * SCALE_LOG2 - total)
                weights[own, cut] = weight.astype(BF16)
                mean = jnp.concatenate([inner[side, :, cut]] * (PATCHES // HEAD_DIM), axis=0)
                slopes[own, cut] = (weight * (pulls[own, cut] - mean)).astype(BF16)

    def mix(pair, slot):
        spread_q, spread_g, _, _, weights, slopes, _ = slot
        at = pair_lanes(pair)
        valid = valid_ref[0, :, at]
        k_one, k_two = halves(qkv_ref[0, WIDTH : 2 * WIDTH, at].astype(F32) * valid, left)
        own_left = left[:GROUP_ROWS]
        for group in range(GROUPS):
            cut = slice(group * GROUP_LANES, (group + 1) * GROUP_LANES)
            start = group * GROUP_ROWS
            rows = slice(start, start + GROUP_ROWS)
            weight = weights[:, cut]
            slope = slopes[:, cut]
            by_value = dot_rows(
                jnp.concatenate([spread_g[0, rows, cut], spread_g[1, rows, cut]], axis=0), weight
            )
            by_value = jnp.where(own_left, by_value[:GROUP_ROWS], by_value[GROUP_ROWS:])
            grads[2 * WIDTH + start : 2 * WIDTH + start + GROUP_ROWS, at] = (
                by_value * valid
            ).astype(BF16)
            by_key = dot_rows(
                jnp.concatenate([spread_q[0, rows, cut], spread_q[1, rows, cut]], axis=0), slope
            )
            by_key = jnp.where(own_left, by_key[:GROUP_ROWS], by_key[GROUP_ROWS:])
            grads[WIDTH + start : WIDTH + start + GROUP_ROWS, at] = (
                by_key * (valid * SCALE)
            ).astype(BF16)
            by_query = dot(jnp.concatenate([k_one[rows], k_two[rows]], axis=0), slope)
            grads[rows, at] = (
                gather_heads(by_query[:GROUP_ROWS], by_query[GROUP_ROWS:], left) * SCALE
            ).astype(BF16)

    pipeline(pairs, slots, score, soften, mix)

    def finish(at):
        if first_layer:
            low_full[:, at] = x_ref[at, :].astype(F32).T.astype(BF16)
        else:
            normal = normalise(x_ref[0, :, at], columns_prev)
            inputs = normal * wide(columns_prev[5], CHUNK) + wide(columns_prev[3], CHUNK)
            low_full[:, at] = inputs.astype(BF16)
        grad = grad_full[:, at] + dot(w_in[...], grads[:, at])
        if first_layer:
            gx_out[at, :] = grad.T.astype(BF16)
        else:
            gx_out[0, :, at] = grad
            add_gradient(grad, normal, valid_ref[0, :, at], scratch)

    chunks(lanes, finish)
    for part in range(3):
        rows = slice(part * WIDTH, (part + 1) * WIDTH)
        weights_out[(part + 1) * WIDTH : (part + 2) * WIDTH, :] += dot_rows(
            low_full[...], grads[rows, :]
        )
    if first_layer:

        @pl.when(step == last)
        def _():
            shares[0].begin()
            for share in shares[1:]:
                share.stages[0].drain()
                share.stages[1].finish()
            shares[0].stages[0].receive()
            shares[0].add()
            shares[0].stages[1].start()
            shares[0].stages[0].drain()
            shares[0].stages[1].finish()

    else:
        if start:
            pl.when(step == last)(rows_sent.finish)
        if closes:
            gradient_sums(step, sizes, columns_prev, back_out, rows_out, scratch)
        else:

            @pl.when(step == last)
            def _():
                made[0] = scratch[0][...]
                made[1] = scratch[1][...]


def fixed(shape):
    return pl.BlockSpec(shape, lambda step: (0,) * len(shape))


def blocked(array, first=0):
    return pl.BlockSpec((1,) + array.shape[1:], lambda step: (first + step, 0, 0))


def layer_of(array, layer):
    shape = (1,) + array.shape[1:]
    return pl.BlockSpec(shape, lambda step: (layer,) + (0,) * (len(shape) - 1))


def rows_of(lanes):
    return pl.BlockSpec((lanes, WIDTH), lambda step: (step, 0))


ANY = pl.BlockSpec(memory_space=pl.ANY)


def shaped(shape, dtype=F32):
    return jax.ShapeDtypeStruct(shape, dtype)


def call(
    body, blocks, ins, in_specs, outs, out_specs, scratch, flops, collective=None, aliases=None
):
    arrays = list(ins) + (list(outs) if isinstance(outs, tuple) else [outs])
    size = sum(math.prod(a.shape) * a.dtype.itemsize for a in arrays)
    return pl.pallas_call(
        body,
        grid=(blocks,),
        in_specs=in_specs,
        out_specs=out_specs,
        out_shape=outs,
        scratch_shapes=scratch,
        input_output_aliases=aliases or {},
        compiler_params=pltpu.CompilerParams(
            dimension_semantics=("arbitrary",),
            vmem_limit_bytes=VMEM_BYTES,
            collective_id=collective,
            has_side_effects=collective is not None,
        ),
        cost_estimate=pl.CostEstimate(flops=flops, bytes_accessed=size, transcendentals=0),
    )(*ins)


STAT_SCRATCH = [
    pltpu.VMEM((WIDTH, WIDTH), F32),
    pltpu.VMEM((WIDTH, WIDTH), F32),
    pltpu.VMEM((WIDTH, WIDTH), F32),
    pltpu.VMEM((8, WIDTH), F32),
]
FORWARD_SLOT = [
    pltpu.VMEM((2, WIDTH, SPREAD), BF16),
    pltpu.VMEM((PAIR, SPREAD), F32),
    pltpu.VMEM((PAIR, SPREAD), BF16),
]
BACKWARD_SLOT = [
    pltpu.VMEM((2, WIDTH, SPREAD), BF16),
    pltpu.VMEM((2, WIDTH, SPREAD), BF16),
    pltpu.VMEM((PAIR, SPREAD), F32),
    pltpu.VMEM((PAIR, SPREAD), F32),
    pltpu.VMEM((PAIR, SPREAD), BF16),
    pltpu.VMEM((PAIR, SPREAD), BF16),
    pltpu.VMEM((2, HEAD_DIM, SPREAD), F32),
]
SUM_SCRATCH = [pltpu.VMEM((WIDTH, WIDTH), F32), pltpu.VMEM((WIDTH, WIDTH), F32)]


def swap_scratch(sizes):
    devices = sizes[0] * sizes[1]
    return [
        pltpu.VMEM((devices, 8, WIDTH), F32),
        pltpu.SemaphoreType.DMA,
        pltpu.SemaphoreType.DMA,
    ]


def head_gradient(sizes, inner, parts, batch_cotangent):
    sources, part, _, width = parts[0].shape
    series, horizon = batch_cotangent.shape[1:]
    group = lax.axis_index("dp") // inner
    cotangent = batch_cotangent
    if cotangent.shape[0] != sources:
        cotangent = lax.dynamic_slice_in_dim(cotangent, group * sources, sources, 0)
    at_once = 4
    shape = shaped((horizon, part * width), BF16)
    return call(
        head_gradient_body,
        sources // at_once,
        (*parts, cotangent),
        [
            pl.BlockSpec((at_once,) + rows.shape[1:], lambda step: (step, 0, 0, 0))
            for rows in parts
        ]
        + [pl.BlockSpec((at_once, series, horizon), lambda step: (step, 0, 0))],
        shape,
        fixed(shape.shape),
        [pltpu.VMEM((part, width, horizon), F32)],
        2 * sources * series * part * width * horizon,
    )


def spread_head(sizes, inner, rows):
    gathered = lax.all_gather(rows, "dp", axis=0)
    outer = sizes[0] // inner
    if outer > 1:
        gathered = jnp.sum(gathered.reshape((outer, inner) + rows.shape).astype(F32), axis=0)
    return gathered


def finish_outputs(rows, summed, tiles, layers, hidden):
    inner, horizon, columns = rows.shape
    at_once = math.gcd(inner, 4)
    shapes = (
        shaped((horizon, inner * columns)),
        shaped((layers, 3, WIDTH, WIDTH)),
        shaped((layers, WIDTH, WIDTH)),
        shaped((layers, WIDTH, hidden)),
        shaped((layers, hidden, WIDTH)),
        shaped((layers, 2, WIDTH)),
        shaped((layers, 2, WIDTH)),
    )
    head, *others = call(
        functools.partial(widen_body, layers),
        inner // at_once,
        (rows, summed, *tiles),
        [
            pl.BlockSpec((at_once, horizon, columns), lambda step: (step, 0, 0)),
            fixed(summed.shape),
        ]
        + [fixed(tile.shape) for tile in tiles],
        shapes,
        (pl.BlockSpec((horizon, at_once * columns), lambda step: (0, step)),)
        + tuple(fixed(shape.shape) for shape in shapes[1:]),
        [],
        1,
    )
    return *others, head.T


def per_device(
    sizes,
    embedded_segments,
    history_durations,
    segment_seen_indicator,
    query_key_value_matrices,
    mixing_result_matrices,
    first_dense_matrices,
    second_dense_matrices,
    batchnorm_scales,
    batchnorm_offsets,
    readout_matrix,
    prediction_cotangent,
):
    series, patches, width = embedded_segments.shape
    layers = query_key_value_matrices.shape[0]
    hidden = first_dense_matrices.shape[2]
    block = math.gcd(series, 16)
    blocks = series // block
    lanes = block * patches
    tokens = series * patches
    positions = jnp.arange(patches, dtype=jnp.int32)
    first_valid = patches - ((history_durations - 16) // 8 + 2)
    valid = (positions[None, :] >= first_valid[:, None]) & (segment_seen_indicator > 0)
    valid_rows = valid.astype(F32).reshape(blocks, 1, lanes)
    embedded = embedded_segments.reshape(tokens, width)
    horizon = readout_matrix.shape[1]
    readout_own = readout_matrix.T
    inner = math.gcd(sizes[0], patches // sizes[1])
    wide_f32 = shaped((blocks, width, lanes))
    columns_shape = shaped((6, WIDTH, WIDTH))
    back_shape = shaped((2, WIDTH, WIDTH))
    tile_shape = shaped((8, WIDTH))
    norm_specs = [fixed(batchnorm_scales.shape), fixed(batchnorm_offsets.shape)]
    half_rows = readout_matrix.shape[0]
    flat_spec, own_spec, other_spec = head_specs(horizon, half_rows, patches, series)
    pm_f32 = shaped((patches, series, width))
    pm_bf16 = shaped((patches, series, width), BF16)
    series_spec = pl.BlockSpec((patches, block, width), lambda step: (0, step, 0))
    weights_shape = shaped((4 * width, width))
    swap = swap_scratch(sizes)
    kept = []
    columns = None
    state = embedded
    batch_cotangent = lax.all_gather(prediction_cotangent, ("dp", "patch"), axis=0)
    for layer in range(layers):
        first = layer == 0
        qkv_shape = shaped((blocks, 3 * width, lanes), BF16)
        o_shape = shaped((blocks, width, lanes), BF16)
        lse_shape = shaped((blocks, block, SPREAD))
        ins = (state, readout_own) if first else (state, columns)
        specs = [rows_of(lanes), ANY] if first else [blocked(state), fixed(columns.shape)]
        makes_head = layer == layers - 1
        attended, qkv, mixed, lse, columns_one, *extra = call(
            functools.partial(attention_forward_body, sizes, layer, first, makes_head),
            blocks,
            ins
            + (
                query_key_value_matrices,
                mixing_result_matrices,
                valid_rows,
                batchnorm_scales,
                batchnorm_offsets,
            )
            + ((prediction_cotangent, readout_own, readout_other) if makes_head else ()),
            specs
            + [layer_of(query_key_value_matrices, layer), layer_of(mixing_result_matrices, layer)]
            + [blocked(valid_rows)]
            + norm_specs
            + (
                [fixed(prediction_cotangent.shape), own_spec, other_spec] if makes_head else []
            ),
            (wide_f32, qkv_shape, o_shape, lse_shape, columns_shape)
            + ((shaped(readout_own.shape, BF16),) if first else ())
            + ((pm_f32,) if makes_head else ()),
            (
                blocked(wide_f32),
                blocked(qkv_shape),
                blocked(o_shape),
                blocked(lse_shape),
                fixed(columns_shape.shape),
            )
            + ((ANY,) if first else ())
            + ((flat_spec,) if makes_head else ()),
            FORWARD_SLOT * 2
            + [
                pltpu.VMEM((width, lanes), F32),
                pltpu.VMEM((width, lanes), F32),
                pltpu.VMEM((lanes, width), BF16),
                pltpu.VMEM((block, SPREAD), F32),
                pltpu.VMEM((block, SPREAD), F32),
                pltpu.VMEM((3 * width, width), BF16),
                pltpu.VMEM((width, width), BF16),
            ]
            + STAT_SCRATCH
            + swap
            + ([pltpu.SemaphoreType.DMA((2,))] if first else []),
            20 * 10**9,
            2 * layer,
        )
        if first:
            readout_other, *extra = extra
        if makes_head:
            (grad_rows,) = extra
        summed, columns_two = call(
            functools.partial(feed_forward_body, sizes, layer),
            blocks,
            (
                attended,
                columns_one,
                first_dense_matrices,
                second_dense_matrices,
                valid_rows,
                batchnorm_scales,
                batchnorm_offsets,
            ),
            [
                blocked(attended),
                fixed(columns_one.shape),
                layer_of(first_dense_matrices, layer),
                layer_of(second_dense_matrices, layer),
                blocked(valid_rows),
            ]
            + norm_specs,
            (wide_f32, columns_shape),
            (blocked(wide_f32), fixed(columns_shape.shape)),
            [pltpu.VMEM((hidden, width), BF16), pltpu.VMEM((width, hidden), BF16)]
            + STAT_SCRATCH
            + swap,
            10 * 10**9,
            2 * layer + 1,
        )
        kept.append(
            (state, columns, attended, qkv, mixed, lse, columns_one, summed, columns_two)
        )
        state, columns = summed, columns_two

    sources = inner * sizes[1]
    own_patches = patches // sources
    early = max(5 * blocks // 9, 1)
    early_shape, late_shape = [
        shaped((sources, own_patches, count, width), BF16)
        for count in (early * block, series - early * block)
    ]
    flat, grad_state, back_two, rows_two = call(
        functools.partial(turn_body, sizes),
        blocks,
        (state, columns, valid_rows, grad_rows),
        [blocked(state), fixed(columns.shape), blocked(valid_rows), series_spec],
        (pm_bf16, wide_f32, back_shape, tile_shape),
        (series_spec, blocked(wide_f32), fixed(back_shape.shape), fixed(tile_shape.shape)),
        [pltpu.VMEM((lanes, width), F32)] + SUM_SCRATCH + swap,
        10**9,
        2 * layers,
    )
    out_shape = shaped((series, horizon), BF16)
    row_sems = [pltpu.SemaphoreType.DMA((2,))]

    weights, tiles = [], []
    for layer in reversed(range(layers)):
        first = layer == 0
        state, columns, attended, qkv, mixed, lse, columns_one, summed, columns_two = kept[layer]
        ships = layer == layers - 1
        grad_normed, feed_weights, back_one, rows_one, *extra = call(
            functools.partial(feed_backward_body, sizes, inner, ships),
            blocks,
            (
                grad_state,
                summed,
                attended,
                columns_two,
                back_two,
                columns_one,
                second_dense_matrices,
                first_dense_matrices,
                valid_rows,
            )
            + ((flat, readout_own, readout_other, flat) if ships else ()),
            [
                blocked(grad_state),
                blocked(summed),
                blocked(attended),
                fixed(columns_two.shape),
                fixed(back_two.shape),
                fixed(columns_one.shape),
                layer_of(second_dense_matrices, layer),
                layer_of(first_dense_matrices, layer),
                blocked(valid_rows),
            ]
            + ([flat_spec, own_spec, other_spec, ANY] if ships else []),
            (wide_f32, weights_shape, back_shape, tile_shape)
            + ((out_shape, early_shape) if ships else ()),
            (
                blocked(wide_f32),
                fixed(weights_shape.shape),
                fixed(back_shape.shape),
                fixed(tile_shape.shape),
            )
            + ((fixed(out_shape.shape), ANY) if ships else ()),
            ([pltpu.VMEM(out_shape.shape, F32)] if ships else [])
            + [
                pltpu.VMEM((hidden, lanes), BF16),
                pltpu.VMEM((width, lanes), BF16),
                pltpu.VMEM((width, lanes), BF16),
                pltpu.VMEM((hidden, lanes), BF16),
                pltpu.VMEM((hidden, width), BF16),
            ]
            + SUM_SCRATCH
            + swap
            + (row_sems if ships else []),
            20 * 10**9,
            2 * layers + 1 + 2 * layer,
        )
        if ships:
            predictions, early_rows = extra
        tiles = [rows_one, rows_two] + tiles
        scratch = BACKWARD_SLOT * 2 + [
            pltpu.VMEM((width, lanes), BF16),
            pltpu.VMEM((width, lanes), F32),
            pltpu.VMEM((width, lanes), F32),
            pltpu.VMEM((lanes, width), BF16),
            pltpu.VMEM((lanes, width), BF16),
            pltpu.VMEM((3 * width, lanes), BF16),
            pltpu.VMEM((width, 3 * width), BF16),
        ]
        ins = (
            grad_normed,
            attended,
            qkv,
            mixed,
            lse,
            valid_rows,
            columns_one,
            back_one,
            mixing_result_matrices,
            query_key_value_matrices,
            state,
        )

        def specs_from(at):
            return [
                blocked(grad_normed, at),
                blocked(attended, at),
                blocked(qkv, at),
                blocked(mixed, at),
                blocked(lse, at),
                blocked(valid_rows, at),
                fixed(columns_one.shape),
                fixed(back_one.shape),
                layer_of(mixing_result_matrices, layer),
                layer_of(query_key_value_matrices, layer),
            ]

        if first:
            others = tuple(weights) + (feed_weights,)
            devices = inner * sizes[1]
            summed_shape = shaped(
                (1 + len(others),) + weights_shape.shape, sharing_dtype(devices)
            )
            input_grad, summed_weights = call(
                functools.partial(attention_backward_body, sizes, inner, True, True, True, 0),
                blocks,
                ins + others,
                specs_from(0) + [rows_of(lanes)] + [fixed(weights_shape.shape)] * len(others),
                (shaped((tokens, width), BF16), summed_shape),
                (rows_of(lanes), ANY),
                scratch
                + [pltpu.VMEM(weights_shape.shape, F32)]
                + sharing_scratch(devices) * (1 + len(others)),
                50 * 10**9,
                2 * layers + 2 + 2 * layer,
            )
        else:
            start = early * block if ships and early < blocks else 0
            cut = (blocks + 1) // 2 if start else 0
            carried = ()
            if start:
                grad_state, attention_weights, sums, late_rows = call(
                    functools.partial(
                        attention_backward_body, sizes, inner, False, True, False, start
                    ),
                    cut,
                    ins + (columns, flat),
                    specs_from(0) + [blocked(state), fixed(columns.shape), ANY],
                    (wide_f32, weights_shape, back_shape, late_shape),
                    (
                        blocked(wide_f32),
                        fixed(weights_shape.shape),
                        fixed(back_shape.shape),
                        ANY,
                    ),
                    scratch + SUM_SCRATCH + swap + row_sems,
                    25 * 10**9,
                    4 * layers + 1,
                )
                carried = (grad_state, attention_weights, sums)
                parts = (early_rows, late_rows)
            elif ships:
                parts = (early_rows,)
            if ships:
                head_rows = head_gradient(sizes, inner, parts, batch_cotangent)
                (*carried, grad_normed), head_rows = lax.optimization_barrier(
                    ((*carried, grad_normed), head_rows)
                )
                head_rows = spread_head(sizes, inner, head_rows)
            grad_state, attention_weights, back_two, rows_two = call(
                functools.partial(
                    attention_backward_body, sizes, inner, False, not carried, True, 0
                ),
                blocks - cut,
                (grad_normed,) + ins[1:] + (columns, *carried),
                specs_from(cut)
                + [blocked(state, cut), fixed(columns.shape)]
                + (
                    [ANY, fixed(weights_shape.shape), fixed(back_shape.shape)]
                    if carried
                    else []
                ),
                (wide_f32, weights_shape, back_shape, tile_shape),
                (
                    blocked(wide_f32, cut),
                    fixed(weights_shape.shape),
                    fixed(back_shape.shape),
                    fixed(tile_shape.shape),
                ),
                scratch + SUM_SCRATCH + swap,
                25 * 10**9,
                2 * layers + 2 + 2 * layer,
                {len(ins) + 1: 0} if carried else None,
            )
            weights += [feed_weights, attention_weights]
    if devices < sizes[0] * sizes[1]:
        summed_weights = lax.psum(summed_weights.astype(F32), ("dp", "patch")) / devices
    return (
        predictions,
        input_grad.reshape(series, patches, width),
        *finish_outputs(head_rows, summed_weights, tiles, layers, hidden),
    )


def solution(mesh):
    placed = (
        P(("dp", "patch"), None, None),
        P(("dp", "patch")),
        P(("dp", "patch"), None),
        P(),
        P(),
        P(),
        P(),
        P(),
        P(),
        P("patch", None),
        P(("dp", "patch"), None),
    )
    sizes = (mesh.shape["dp"], mesh.shape["patch"])
    return jax.shard_map(
        functools.partial(per_device, sizes),
        mesh=mesh,
        in_specs=placed,
        out_specs=(
            P(("dp", "patch"), None),
            P(("dp", "patch"), None, None),
            P(),
            P(),
            P(),
            P(),
            P(),
            P(),
            P("patch", None),
        ),
        check_vma=False,
    )
```

time: 1950 us -> 368 us (0.19)
  matrix products: 618 us -> 0 us
  blocking collectives: 486 us -> 0 us
  waiting for transfers between devices: 445 us -> 1.58 us
  Pallas kernels: 0 us -> 346 us
  other arithmetic: 191 us -> 1.54 us
  local copies, waits for them, and re-layouts: 166 us -> 2.92 us
    dot_general x165 -> x0, matrix products: 618 us -> none  [the longest x36 121 us: masked_scores(): jnp.einsum('bqhe,bkhe->bhqk', query_heads, key_heads, preferred_element_t...]
    psum x12 -> x0, blocking collectives: 484 us -> none  [the longest x4 162 us: norm_forward(): lax.psum((jnp.sum(weighted * values, axis=(0, 1)), own_count), ('dp', 'pa...]
    psum x2 -> x0, waiting for transfers between devices: 445 us -> none  [the longest x1 343 us: per_device(): grad_head = lax.psum(head_term, 'dp')]
    pallas_call x0 -> x12, Pallas kernels: none -> 346 us  [call(): pl.pallas_call(body, grid=(blocks,), in_specs=in_specs, out_specs=out_spe...]
    convert_element_type x22 -> x0, other arithmetic: 80.3 us -> none  [the longest x18 63.8 us: attend_backward(): (probabilities * (grad_weights - inner_sum)).astype(jnp.bfloat16)]
    reduce_sum x26 -> x0, other arithmetic: 79.6 us -> none  [the longest x18 53.3 us: attend_forward(): total_weight = jnp.sum(exponential, axis=-1, keepdims=True)]
    while x8 -> x0, local copies, waits for them, and re-layouts: 43.8 us -> none  [series_blocks(): result = lax.map(lambda block_items: function(*block_items), stacked)]
    another operation x10 -> x0, local copies, waits for them, and re-layouts: 28 us -> none
  transfers between devices with their start and end apart: 5 -> 2, of which waited for: 2 -> 1; matrix products, arithmetic and copies ran while one was open for 39% -> 1% of each run, Pallas kernels for 0% -> 90%
where the time goes in v1:
time: 368 us; the launch traced here: 366 us
  Pallas kernels  346 us (94%)
  between operations  14.2 us (4%)
    pallas_call x12, Pallas kernels, call(): pl.pallas_call(body, grid=(blocks,), in_specs=in_specs, out_specs=out_spe...  346 us
  transfers between devices with their start and end apart: 2, of which 1 were waited for; matrix products, arithmetic and copies ran while one was open for 1% of the time, Pallas kernels for 90%

profile of v1, /device:TPU:0, one launch (start us, length us, event | category | flops | bytes accessed | tf_op | source)
XLA Modules:
  0.0 366.4 jit_solution(8989457039255643621)
XLA Ops:
  7.2 0.0 all-gather.5.cloned.1.call-start
  7.2 0.7 all-gather.5.cloned.1.call-update
  7.9 0.0 all-gather.7.cloned.1.call-start
  8.0 0.7 add_subtract_fusion
  8.6 0.9 fusion.1
  9.5 0.1 copy.22
  9.6 0.7 reshape.38.refs_4_.valid_ref.refs_8_.refs_5_
  10.3 33.9 %shard_map.178 = (f32[9,128,1024]{2,1,0:T(8,128)}, bf16[9,384,1024]{2,1,0:T(8,128)(2,1)}, bf16[9,128,1024]{2,1,0:T(8,128)(2,1)}, f32[9,16,1024]{2,1,0:T(8,128)},...) custom-call(bf16[9216,128]{1,0:T(8,128)(2,1)} %bitcast.13, bf16[720,4096]{1,0:T(8,128)(2,1)} %bitcast.10, ...), custom_call_target="tpu_custom_call" | custom-call | flops 20000000000 | bytes 29597696 | tf_op jit(solution)/shard_map/pallas_call | solution.py:1023
  44.3 21.0 %shard_map.179 = (f32[9,128,1024]{2,1,0:T(8,128)}, f32[6,128,128]{2,1,0:T(8,128)}) custom-call(f32[9,128,1024]{2,1,0:T(8,128)} %get-tuple-element.61.h_ref.refs_2_.refs_1_, f32[6,128,128]{2,1,0:T(8,128)} %get-tuple-element.62.columns.refs_5_.refs_6_, bf16[2,128,256]{2,1,0:T(8,128)(2,1)} %refs_7_.5, bf16[2,256,128]{2,1,0:T(8,128)(2,1)} %refs_6_.7, ...), custom_call_target="tpu_custom_call" | custom-call | flops 10000000000 | bytes 10526720 | tf_op jit(solution)/shard_map/pallas_call | solution.py:1023
  65.3 37.7 %shard_map.180 = (f32[9,128,1024]{2,1,0:T(8,128)}, bf16[9,384,1024]{2,1,0:T(8,128)(2,1)}, bf16[9,128,1024]{2,1,0:T(8,128)(2,1)}, f32[9,16,1024]{2,1,0:T(8,128)},...) custom-call(f32[9,128,1024]{2,1,0:T(8,128)} %get-tuple-element.63.refs_0_.refs_10_.refs_1_, ...), custom_call_target="tpu_custom_call" | custom-call | flops 20000000000 | bytes 37276160 | tf_op jit(solution)/shard_map/pallas_call | solution.py:1023
  103.0 18.5 %shard_map.181 = (f32[9,128,1024]{2,1,0:T(8,128)}, f32[6,128,128]{2,1,0:T(8,128)}) custom-call(f32[9,128,1024]{2,1,0:T(8,128)} %get-tuple-element.66.h_ref.refs_2_.refs_1_, f32[6,128,128]{2,1,0:T(8,128)} %get-tuple-element.67.columns.refs_5_.refs_6_, bf16[2,128,256]{2,1,0:T(8,128)(2,1)} %refs_7_.5, bf16[2,256,128]{2,1,0:T(8,128)(2,1)} %refs_6_.7, ...), custom_call_target="tpu_custom_call" | custom-call | flops 10000000000 | bytes 10526720 | tf_op jit(solution)/shard_map/pallas_call | solution.py:1023
  121.5 22.8 %shard_map.182 = (bf16[64,144,128]{2,1,0:T(8,128)(2,1)}, f32[9,128,1024]{2,1,0:T(8,128)}, f32[2,128,128]{2,1,0:T(8,128)}, f32[8,128]{1,0:T(8,128)}) custom-call(f32[9,128,1024]{2,1,0:T(8,128)} %get-tuple-element.68.f_ref.refs_1_, f32[6,128,128]{2,1,0:T(8,128)} %get-tuple-element.69.columns.refs_3_, f32[9,1,1024]{2,1,0:T(1,128)} %reshape.38.refs_4_.valid_ref.refs_8_.refs_5_, ...), custom_call_target="tpu_custom_call" | custom-call | flops 1000000000 | bytes 17080320 | tf_op jit(solution)/shard_map/pallas_call | solution.py:1023
  144.4 47.7 %shard_map.183 = (f32[9,128,1024]{2,1,0:T(8,128)}, f32[512,128]{1,0:T(8,128)}, f32[2,128,128]{2,1,0:T(8,128)}, f32[8,128]{1,0:T(8,128)}, bf16[144,720]{1,0:T(8,128)(2,1)}, /*index=5*/bf16[32,2,80,128]{3,2,1,0:T(8,128)(2,1)}) custom-call(f32[9,128,1024]{2,1,0:T(8,128)} %get-tuple-element.71.refs_0_, f32[9,128,1024]{2,1,0:T(8,128)} %get-tuple-element.68.f_ref.refs_1_, ...), custom_call_target="tpu_custom_call" | custom-call | flops 20000000000 | bytes 38521344 | tf_op jit(solution)/shard_map/pallas_call | solution.py:1023
  192.0 27.0 %shard_map.184 = (f32[9,128,1024]{2,1,0:T(8,128)}, f32[512,128]{1,0:T(8,128)}, f32[2,128,128]{2,1,0:T(8,128)}, bf16[32,2,64,128]{3,2,1,0:T(8,128)(2,1)}) custom-call(f32[9,128,1024]{2,1,0:T(8,128)} %get-tuple-element.85.refs_0_, f32[9,128,1024]{2,1,0:T(8,128)} %get-tuple-element.66.h_ref.refs_2_.refs_1_, bf16[9,384,1024]{2,1,0:T(8,128)(2,1)} %get-tuple-element.76.refs_2_, ...), custom_call_target="tpu_custom_call" | custom-call | flops 24999999488 | bytes 33918976 | tf_op jit(solution)/shard_map/pallas_call | solution.py:1023
  219.0 0.0 all-gather.5.cloned.1.call-done
  219.1 8.9 %shard_map.185 = bf16[720,256]{1,0:T(8,128)(2,1)} custom-call(bf16[32,2,80,128]{3,2,1,0:T(8,128)(2,1)} %get-tuple-element.83.refs_0_, bf16[32,2,64,128]{3,2,1,0:T(8,128)(2,1)} %get-tuple-element.84.refs_1_, bf16[32,144,720]{2,1,0:T(8,128)(2,1)} %bitcast.6), custom_call_target="tpu_custom_call" | custom-call | flops 1698693120 | bytes 9363456 | tf_op jit(solution)/shard_map/pallas_call | solution.py:1023
  228.0 0.0 all-gather.7.cloned.1.call-update
  228.0 34.8 %shard_map.186 = (f32[9,128,1024]{2,1,0:T(8,128)}, f32[512,128]{1,0:T(8,128)}, f32[2,128,128]{2,1,0:T(8,128)}, f32[8,128]{1,0:T(8,128)}) custom-call(f32[9,128,1024]{2,1,0:T(8,128)} %get-tuple-element.85.refs_0_, f32[9,128,1024]{2,1,0:T(8,128)} %get-tuple-element.66.h_ref.refs_2_.refs_1_, ...), custom_call_target="tpu_custom_call", output_to_operand_aliasing={{0}: (12, {})} | custom-call | flops 24999999488 | bytes 35627008 | tf_op jit(solution)/shard_map/pallas_call | solution.py:1023
  262.8 22.7 %shard_map.187 = (f32[9,128,1024]{2,1,0:T(8,128)}, f32[512,128]{1,0:T(8,128)}, f32[2,128,128]{2,1,0:T(8,128)}, f32[8,128]{1,0:T(8,128)}) custom-call(f32[9,128,1024]{2,1,0:T(8,128)} %get-tuple-element.89.refs_0_, f32[9,128,1024]{2,1,0:T(8,128)} %get-tuple-element.63.refs_0_.refs_10_.refs_1_, f32[9,128,1024]{2,1,0:T(8,128)} %get-tuple-element.61.h_ref.refs_2_.refs_1_, ...), custom_call_target="tpu_custom_call" | custom-call | flops 20000000000 | bytes 20488192 | tf_op jit(solution)/shard_map/pallas_call | solution.py:1023
  285.5 62.9 %shard_map.188 = (bf16[9216,128]{1,0:T(8,128)(2,1)}, bf16[4,512,128]{2,1,0:T(8,128)(2,1)}) custom-call(f32[9,128,1024]{2,1,0:T(8,128)} %get-tuple-element.91.refs_0_, f32[9,128,1024]{2,1,0:T(8,128)} %get-tuple-element.61.h_ref.refs_2_.refs_1_, bf16[9,384,1024]{2,1,0:T(8,128)(2,1)} %get-tuple-element.92.refs_2_, ...), custom_call_target="tpu_custom_call" | custom-call | flops 49999998976 | bytes 26316800 | tf_op jit(solution)/shard_map/pallas_call | solution.py:1023
  348.5 0.0 copy-start.1
  348.5 0.0 copy-start
  348.5 0.9 all-gather.7.cloned.1.call-done
  349.4 8.1 %shard_map.189 = (f32[720,4096]{1,0:T(8,128)}, f32[2,3,128,128]{3,2,1,0:T(8,128)}, f32[2,128,128]{2,1,0:T(8,128)}, f32[2,128,256]{2,1,0:T(8,128)}, f32[2,256,128...) custom-call(bf16[16,720,256]{2,1,0:T(8,128)(2,1)} %bitcast.7, ...), custom_call_target="tpu_custom_call" | custom-call | flops 1 | bytes 19288064 | tf_op jit(solution)/shard_map/pallas_call | solution.py:1023
  357.5 0.0 copy-done.1
  357.5 0.7 copy.36
  358.2 0.0 copy-done
  358.2 1.4 copy.37
Async XLA Ops:
  7.2 211.9 %all-gather.5.cloned.1.call-start = ((), (), s32[]{:S(2)}) async-start(), calls=%async_computation | async-start | bytes 7299072 | tf_op jit(solution)/shard_map/all_gather | solution.py:1180
  7.9 341.5 %all-gather.7.cloned.1.call-start = ((), (), s32[]{:S(2)}) async-start(), calls=%async_computation.1 | async-start | bytes 6266880 | tf_op jit(solution)/shard_map/all_gather | solution.py:1099
  348.5 9.0 %copy-start.1 = (bf16[144,720]{1,0:T(8,128)(2,1)S(1)}, bf16[144,720]{1,0:T(8,128)(2,1)}, u32[]{:S(2)}) copy-start(bf16[144,720]{1,0:T(8,128)(2,1)} %get-tuple-element.122) | copy-start | bytes 622084
  348.5 9.7 %copy-start = (bf16[9216,128]{1,0:T(8,128)(2,1)S(1)}, bf16[9216,128]{1,0:T(8,128)(2,1)}, u32[]{:S(2)}) copy-start(bf16[9216,128]{1,0:T(8,128)(2,1)} %get-tuple-element.99) | copy-start | bytes 7077892
Sparse Core Ops, SparseCore 0:
  10.9 75.5 all-gather.4
  228.1 121.2 all-gather.6

commit v2 on v1

--- a/solution.py
+++ b/solution.py
@@ -38,6 +38,10 @@
     return lax.dot_general(left, right, (((1,), (1,)), ((), ())), preferred_element_type=F32)
 
 
+def at_layer(ref, layer):
+    return ref.at[pl.ds(layer, 1)]
+
+
 def turn(matrix):
     return matrix.astype(F32).T.astype(matrix.dtype)
 
@@ -214,19 +218,25 @@
 
 
 class Spread:
-    def __init__(self, sizes, inner, source, target, like, send, arrive):
-        self.sizes, self.inner = sizes, inner
+    def __init__(self, sizes, inner, source, target, like, send, arrive, pieces=1):
+        self.sizes, self.inner, self.pieces = sizes, inner, pieces
         self.source, self.target, self.like = source, target, like
         self.send, self.arrive = send, arrive
         self.devices = inner * sizes[1]
         self.group, self.own = own_part(sizes, inner)
 
     def start(self):
-        def begin(offset, carry):
+        def piece(ref, index):
+            size = ref.shape[0] // self.pieces
+            return ref if self.pieces == 1 else ref.at[pl.ds(index * size, size)]
+
+        def begin(count, carry):
+            index = (count - 1) // (self.devices - 1)
+            offset = count - index * (self.devices - 1)
             other = lax.rem(self.own + offset, self.devices)
             pltpu.make_async_remote_copy(
-                src_ref=self.source(other),
-                dst_ref=self.target(self.own),
+                src_ref=piece(self.source(other), index),
+                dst_ref=piece(self.target(self.own), index),
                 send_sem=self.send,
                 recv_sem=self.arrive,
                 device_id=(
@@ -240,7 +250,7 @@
         pltpu.make_async_copy(
             self.source(self.own), self.target(self.own), self.arrive
         ).start()
-        lax.fori_loop(1, self.devices, begin, 0)
+        lax.fori_loop(1, self.pieces * (self.devices - 1) + 1, begin, 0)
 
     def receive(self):
         await_bytes(self.like(self.devices), self.arrive)
@@ -321,6 +331,21 @@
         lambda places: slots.at[pl.ds(0, places)],
         send,
         arrive,
+        part,
+    )
+
+
+def partner_copy(sizes, inner, partial, got, sems):
+    chip = lax.axis_index("dp")
+    half = lax.rem(chip, inner) // (inner // 2)
+    other = chip + (1 - 2 * half) * (inner // 2)
+    return half, pltpu.make_async_remote_copy(
+        src_ref=partial.at[1 - half],
+        dst_ref=got,
+        send_sem=sems.at[0],
+        recv_sem=sems.at[1],
+        device_id=(other, lax.axis_index("patch")),
+        device_id_type=pl.DeviceIdType.MESH,
     )
 
 
@@ -358,7 +383,7 @@
         tiles[own, 0:1, :] = pivot[...].T[0:1, :] + shift / total
         tiles[own, 1:2, :] = square - shift * shift / total
         tiles[own, 2:3, :] = total
-        tiles[own, 3:8, :] = jnp.zeros((5, WIDTH), F32)
+        tiles[own, 3:4, :] = total
         swap_tiles(sizes, tiles, send, arrive)
         means, spreads, counts = tiles[:, 0, :], tiles[:, 1, :], tiles[:, 2, :]
         total = jnp.sum(counts, axis=0, keepdims=True)
@@ -395,7 +420,6 @@
         own = lax.axis_index("dp") * sizes[1] + lax.axis_index("patch")
         tiles[own, 0:1, :] = jnp.sum(by_normal[...].T, axis=0, keepdims=True)
         tiles[own, 1:2, :] = jnp.sum(plain[...].T, axis=0, keepdims=True)
-        tiles[own, 2:8, :] = jnp.zeros((6, WIDTH), F32)
         swap_tiles(sizes, tiles, send, arrive)
         summed = jnp.sum(tiles[...], axis=0)
         rows_out[...] = summed
@@ -440,6 +464,7 @@
     size = len(FORWARD_SLOT)
     slots, refs = (refs[:size], refs[size : 2 * size]), refs[2 * size :]
     (x_full, q_full, k_rows, tops, sums, w_in, w_out), scratch = refs[:7], refs[7:]
+    w_in_ref, w_out_ref = at_layer(w_in_ref, layer), at_layer(w_out_ref, layer)
     step = pl.program_id(0)
     greet(step, sizes)
 
@@ -545,6 +570,7 @@
     sizes, layer, h_ref, columns, w_up_ref, w_down_ref, valid_ref, scales, offsets,
     f_out, columns_out, w_up, w_down, *scratch,
 ):
+    w_up_ref, w_down_ref = at_layer(w_up_ref, layer), at_layer(w_down_ref, layer)
     step = pl.program_id(0)
     greet(step, sizes)
 
@@ -574,16 +600,37 @@
 
 
 def turn_body(
-    sizes, f_ref, columns, valid_ref, gz_ref, flat_out, gx_out, back_out, rows_out, turned,
-    *scratch,
+    sizes, inner, f_ref, columns, valid_ref, gz_ref, flat_out, gx_out, back_out, rows_out,
+    slots_out, turned, sent, row_sems, *scratch,
 ):
     step = pl.program_id(0)
     patches, block = gz_ref.shape[:2]
+    part = slots_out.shape[1]
+    early = sent.shape[0]
     greet(step, sizes)
 
+    def shipment(index):
+        return Spread(
+            sizes,
+            inner // 2,
+            lambda place: sent.at[
+                index, pl.ds(first_patch(sizes, inner // 2, patches, place), part)
+            ],
+            lambda slot: slots_out.at[
+                slot, :, pl.ds(pl.multiple_of(index * block, block), block)
+            ],
+            lambda places: slots_out.at[pl.ds(0, places), :, pl.ds(0, block)],
+            row_sems.at[0, index],
+            row_sems.at[1, index],
+        )
+
     @pl.when(step == second_step())
     def _():
         met(sizes)
+
+    @pl.when((step >= 1) & (step <= early))
+    def _():
+        shipment(step - 1).start()
 
     clear_gradient(step, scratch)
     shift = lax.axis_index("patch") * (patches // sizes[1])
@@ -606,6 +653,15 @@
     for patch in range(patches):
         turned[rows_at(patch), :] = gz_ref[patch]
     chunks(f_ref.shape[-1], take)
+
+    @pl.when(step < early)
+    def _():
+        sent[step] = flat_out[...]
+
+    @pl.when(step == pl.num_programs(0) - 1)
+    def _():
+        for index in range(early):
+            shipment(index).finish()
 
     gradient_sums(step, sizes, columns, back_out, rows_out, scratch)
 
@@ -654,7 +710,7 @@
     return flat_spec, own_spec, other_spec
 
 
-def head_gradient_body(*refs):
+def head_gradient_body(half, *refs):
     *parts, cotangent, out, total = refs
     step = pl.program_id(0)
 
@@ -677,15 +733,17 @@
     @pl.when(step == pl.num_programs(0) - 1)
     def _():
         for patch in range(part):
-            out[:, patch * width : (patch + 1) * width] = total[patch].T.astype(out.dtype)
+            index, place = divmod(patch, part // 2)
+            lanes = slice(place * width, (place + 1) * width)
+            out[index, :, lanes] = total[patch].T.astype(out.dtype)
 
 
 def widen_body(layers, *refs):
     rows, summed, *tiles = refs[: 2 + 2 * layers]
     out, in_out, out_out, up_out, down_out, gain_out, shift_out = refs[2 + 2 * layers :]
-    for at in range(rows.shape[0]):
-        width = rows.shape[-1]
-        out[:, at * width : (at + 1) * width] = rows[at].astype(out.dtype)
+    width = rows.shape[-1]
+    for at in range(2 * rows.shape[1]):
+        out[:, at * width : (at + 1) * width] = rows[at % 2, at // 2].astype(out.dtype)
 
     @pl.when(pl.program_id(0) == 0)
     def _():
@@ -705,14 +763,23 @@
                 shift_out[layer, norm : norm + 1, :] = tile[1:2, :]
 
 
-def feed_backward_body(sizes, inner, ships, *refs):
+def feed_backward_body(sizes, inner, layer, ships, *refs):
     (gx_ref, f_ref, h_ref, columns_two, back_two, columns_one, w_down, w_up,
      valid_ref), refs = refs[:9], refs[9:]
+    w_down, w_up = at_layer(w_down, layer), at_layer(w_up, layer)
     if ships:
         flat_chunk, readout_own, readout_other, flat, *refs = refs
         gy_out, weights_out, back_out, rows_out, out, slots_out, total, *scratch = refs
         scratch, row_sems = scratch[:-1], scratch[-1]
-        rows_sent = ship_rows(sizes, inner, flat, 0, slots_out, row_sems.at[0], row_sems.at[1])
+        rows_sent = ship_rows(
+            sizes,
+            inner // 2,
+            flat,
+            flat.shape[1] - slots_out.shape[2],
+            slots_out,
+            row_sems.at[0],
+            row_sems.at[1],
+        )
     else:
         gy_out, weights_out, back_out, rows_out, *scratch = refs
     step = pl.program_id(0)
@@ -769,9 +836,11 @@
     gradient_sums(step, sizes, columns_one, back_out, rows_out, scratch)
 
 
-def attention_backward_body(sizes, inner, first_layer, opens, closes, start, *refs):
+def attention_backward_body(sizes, inner, layer, opens, closes, start, *refs):
+    first_layer = layer == 0
     (gy_ref, h_ref, qkv_ref, o_ref, lse_ref, valid_ref, columns_one, back_one, w_out, w_in_ref,
      x_ref), refs = refs[:11], refs[11:]
+    w_out, w_in_ref = at_layer(w_out, layer), at_layer(w_in_ref, layer)
     taken = made = None
     if first_layer:
         ready, (gx_out, summed_out), refs = refs[:3], refs[3:5], refs[5:]
@@ -791,7 +860,7 @@
     else:
         columns_prev, *refs = refs
         if start:
-            flat, *refs = refs
+            partial, *refs = refs
         if not opens:
             _, taken, *refs = refs
             taken, made = (taken, refs[0]), None
@@ -801,11 +870,9 @@
         else:
             gx_out, weights_out, made, *refs = refs
         if start:
-            slots_out, *refs, row_sems = refs
-            rows_sent = ship_rows(
-                sizes, inner, flat, start, slots_out, row_sems.at[0], row_sems.at[1]
-            )
-        count = len(SUM_SCRATCH) + len(swap_scratch(sizes))
+            rows_out, *refs, got, row_sems = refs
+            half, partner = partner_copy(sizes, inner, partial, got, row_sems)
+        count = len(SUM_SCRATCH) + len(swap_scratch(sizes, 2))
         refs, scratch = refs[:-count], refs[-count:]
     size = len(BACKWARD_SLOT)
     slots = refs[:size], refs[size : 2 * size]
@@ -822,7 +889,7 @@
                 for share in shares[1:]:
                     share.begin()
             elif start:
-                rows_sent.start()
+                partner.start()
 
     if first_layer:
 
@@ -980,7 +1047,13 @@
 
     else:
         if start:
-            pl.when(step == last)(rows_sent.finish)
+
+            @pl.when(step == last)
+            def _():
+                partner.wait()
+                total = partial[half].astype(F32) + got[...].astype(F32)
+                rows_out[...] = total.astype(rows_out.dtype)
+
         if closes:
             gradient_sums(step, sizes, columns_prev, back_out, rows_out, scratch)
         else:
@@ -992,16 +1065,11 @@
 
 
 def fixed(shape):
-    return pl.BlockSpec(shape, lambda step: (0,) * len(shape))
+    return pl.BlockSpec(memory_space=pltpu.VMEM)
 
 
 def blocked(array, first=0):
     return pl.BlockSpec((1,) + array.shape[1:], lambda step: (first + step, 0, 0))
-
-
-def layer_of(array, layer):
-    shape = (1,) + array.shape[1:]
-    return pl.BlockSpec(shape, lambda step: (layer,) + (0,) * (len(shape) - 1))
 
 
 def rows_of(lanes):
@@ -1061,10 +1129,10 @@
 SUM_SCRATCH = [pltpu.VMEM((WIDTH, WIDTH), F32), pltpu.VMEM((WIDTH, WIDTH), F32)]
 
 
-def swap_scratch(sizes):
+def swap_scratch(sizes, rows):
     devices = sizes[0] * sizes[1]
     return [
-        pltpu.VMEM((devices, 8, WIDTH), F32),
+        pltpu.VMEM((devices, rows, WIDTH), F32),
         pltpu.SemaphoreType.DMA,
         pltpu.SemaphoreType.DMA,
     ]
@@ -1073,26 +1141,36 @@
 def head_gradient(sizes, inner, parts, batch_cotangent):
     sources, part, _, width = parts[0].shape
     series, horizon = batch_cotangent.shape[1:]
-    group = lax.axis_index("dp") // inner
-    cotangent = batch_cotangent
-    if cotangent.shape[0] != sources:
-        cotangent = lax.dynamic_slice_in_dim(cotangent, group * sources, sources, 0)
+    half = lax.axis_index("dp") // (inner // 2)
     at_once = 4
-    shape = shaped((horizon, part * width), BF16)
-    return call(
+    steps = sources // at_once
+    return pl.pallas_call(
         head_gradient_body,
-        sources // at_once,
-        (*parts, cotangent),
-        [
-            pl.BlockSpec((at_once,) + rows.shape[1:], lambda step: (step, 0, 0, 0))
-            for rows in parts
-        ]
-        + [pl.BlockSpec((at_once, series, horizon), lambda step: (step, 0, 0))],
-        shape,
-        fixed(shape.shape),
-        [pltpu.VMEM((part, width, horizon), F32)],
-        2 * sources * series * part * width * horizon,
-    )
+        grid_spec=pltpu.PrefetchScalarGridSpec(
+            num_scalar_prefetch=1,
+            grid=(steps,),
+            in_specs=[
+                pl.BlockSpec((at_once,) + rows.shape[1:], lambda step, half: (step, 0, 0, 0))
+                for rows in parts
+            ]
+            + [
+                pl.BlockSpec(
+                    (at_once, series, horizon), lambda step, half: (half[0] * steps + step, 0, 0)
+                )
+            ],
+            out_specs=pl.BlockSpec(memory_space=pltpu.VMEM),
+            scratch_shapes=[pltpu.VMEM((part, width, horizon), F32)],
+        ),
+        out_shape=shaped((2, horizon, part // 2 * width), BF16),
+        compiler_params=pltpu.CompilerParams(
+            dimension_semantics=("arbitrary",), vmem_limit_bytes=VMEM_BYTES
+        ),
+        cost_estimate=pl.CostEstimate(
+            flops=2 * sources * series * part * width * horizon,
+            bytes_accessed=2 * sources * series * (part * width + horizon),
+            transcendentals=0,
+        ),
+    )(half.astype(jnp.int32).reshape(1), *parts, batch_cotangent)
 
 
 def spread_head(sizes, inner, rows):
@@ -1105,6 +1183,7 @@
 
 def finish_outputs(rows, summed, tiles, layers, hidden):
     inner, horizon, columns = rows.shape
+    rows = rows.reshape(2, inner // 2, horizon, columns)
     at_once = math.gcd(inner, 4)
     shapes = (
         shaped((horizon, inner * columns)),
@@ -1120,7 +1199,7 @@
         inner // at_once,
         (rows, summed, *tiles),
         [
-            pl.BlockSpec((at_once, horizon, columns), lambda step: (step, 0, 0)),
+            pl.BlockSpec((2, at_once // 2, horizon, columns), lambda step: (0, step, 0, 0)),
             fixed(summed.shape),
         ]
         + [fixed(tile.shape) for tile in tiles],
@@ -1165,7 +1244,7 @@
     wide_f32 = shaped((blocks, width, lanes))
     columns_shape = shaped((6, WIDTH, WIDTH))
     back_shape = shaped((2, WIDTH, WIDTH))
-    tile_shape = shaped((8, WIDTH))
+    tile_shape = shaped((2, WIDTH))
     norm_specs = [fixed(batchnorm_scales.shape), fixed(batchnorm_offsets.shape)]
     half_rows = readout_matrix.shape[0]
     flat_spec, own_spec, other_spec = head_specs(horizon, half_rows, patches, series)
@@ -1173,7 +1252,7 @@
     pm_bf16 = shaped((patches, series, width), BF16)
     series_spec = pl.BlockSpec((patches, block, width), lambda step: (0, step, 0))
     weights_shape = shaped((4 * width, width))
-    swap = swap_scratch(sizes)
+    stat_swap, sum_swap = swap_scratch(sizes, 4), swap_scratch(sizes, 2)
     kept = []
     columns = None
     state = embedded
@@ -1199,7 +1278,7 @@
             )
             + ((prediction_cotangent, readout_own, readout_other) if makes_head else ()),
             specs
-            + [layer_of(query_key_value_matrices, layer), layer_of(mixing_result_matrices, layer)]
+            + [fixed(query_key_value_matrices.shape), fixed(mixing_result_matrices.shape)]
             + [blocked(valid_rows)]
             + norm_specs
             + (
@@ -1228,7 +1307,7 @@
                 pltpu.VMEM((width, width), BF16),
             ]
             + STAT_SCRATCH
-            + swap
+            + stat_swap
             + ([pltpu.SemaphoreType.DMA((2,))] if first else []),
             20 * 10**9,
             2 * layer,
@@ -1252,8 +1331,8 @@
             [
                 blocked(attended),
                 fixed(columns_one.shape),
-                layer_of(first_dense_matrices, layer),
-                layer_of(second_dense_matrices, layer),
+                fixed(first_dense_matrices.shape),
+                fixed(second_dense_matrices.shape),
                 blocked(valid_rows),
             ]
             + norm_specs,
@@ -1261,7 +1340,7 @@
             (blocked(wide_f32), fixed(columns_shape.shape)),
             [pltpu.VMEM((hidden, width), BF16), pltpu.VMEM((width, hidden), BF16)]
             + STAT_SCRATCH
-            + swap,
+            + stat_swap,
             10 * 10**9,
             2 * layer + 1,
         )
@@ -1270,21 +1349,33 @@
         )
         state, columns = summed, columns_two
 
-    sources = inner * sizes[1]
-    own_patches = patches // sources
-    early = max(5 * blocks // 9, 1)
+    sources = inner // 2 * sizes[1]
+    early = max(4 * blocks // 9, 1)
     early_shape, late_shape = [
-        shaped((sources, own_patches, count, width), BF16)
+        shaped((sources, patches // sources, count, width), BF16)
         for count in (early * block, series - early * block)
     ]
-    flat, grad_state, back_two, rows_two = call(
-        functools.partial(turn_body, sizes),
+    rows_shape = shaped((horizon, patches // sources // 2 * width), BF16)
+    flat, grad_state, back_two, rows_two, early_rows = call(
+        functools.partial(turn_body, sizes, inner),
         blocks,
         (state, columns, valid_rows, grad_rows),
         [blocked(state), fixed(columns.shape), blocked(valid_rows), series_spec],
-        (pm_bf16, wide_f32, back_shape, tile_shape),
-        (series_spec, blocked(wide_f32), fixed(back_shape.shape), fixed(tile_shape.shape)),
-        [pltpu.VMEM((lanes, width), F32)] + SUM_SCRATCH + swap,
+        (pm_bf16, wide_f32, back_shape, tile_shape, early_shape),
+        (
+            series_spec,
+            blocked(wide_f32),
+            fixed(back_shape.shape),
+            fixed(tile_shape.shape),
+            ANY,
+        ),
+        [
+            pltpu.VMEM((lanes, width), F32),
+            pltpu.VMEM((early, patches, block, width), BF16),
+            pltpu.SemaphoreType.DMA((2, early)),
+        ]
+        + SUM_SCRATCH
+        + sum_swap,
         10**9,
         2 * layers,
     )
@@ -1297,7 +1388,7 @@
         state, columns, attended, qkv, mixed, lse, columns_one, summed, columns_two = kept[layer]
         ships = layer == layers - 1
         grad_normed, feed_weights, back_one, rows_one, *extra = call(
-            functools.partial(feed_backward_body, sizes, inner, ships),
+            functools.partial(feed_backward_body, sizes, inner, layer, ships),
             blocks,
             (
                 grad_state,
@@ -1318,13 +1409,13 @@
                 fixed(columns_two.shape),
                 fixed(back_two.shape),
                 fixed(columns_one.shape),
-                layer_of(second_dense_matrices, layer),
-                layer_of(first_dense_matrices, layer),
+                fixed(second_dense_matrices.shape),
+                fixed(first_dense_matrices.shape),
                 blocked(valid_rows),
             ]
             + ([flat_spec, own_spec, other_spec, ANY] if ships else []),
             (wide_f32, weights_shape, back_shape, tile_shape)
-            + ((out_shape, early_shape) if ships else ()),
+            + ((out_shape, late_shape) if ships else ()),
             (
                 blocked(wide_f32),
                 fixed(weights_shape.shape),
@@ -1341,13 +1432,15 @@
                 pltpu.VMEM((hidden, width), BF16),
             ]
             + SUM_SCRATCH
-            + swap
+            + sum_swap
             + (row_sems if ships else []),
             20 * 10**9,
             2 * layers + 1 + 2 * layer,
         )
         if ships:
-            predictions, early_rows = extra
+            predictions, late_rows = extra
+            partial = head_gradient(sizes, inner, (early_rows, late_rows), batch_cotangent)
+            grad_normed, partial = lax.optimization_barrier((grad_normed, partial))
         tiles = [rows_one, rows_two] + tiles
         scratch = BACKWARD_SLOT * 2 + [
             pltpu.VMEM((width, lanes), BF16),
@@ -1382,8 +1475,8 @@
                 blocked(valid_rows, at),
                 fixed(columns_one.shape),
                 fixed(back_one.shape),
-                layer_of(mixing_result_matrices, layer),
-                layer_of(query_key_value_matrices, layer),
+                fixed(mixing_result_matrices.shape),
+                fixed(query_key_value_matrices.shape),
             ]
 
         if first:
@@ -1393,7 +1486,7 @@
                 (1 + len(others),) + weights_shape.shape, sharing_dtype(devices)
             )
             input_grad, summed_weights = call(
-                functools.partial(attention_backward_body, sizes, inner, True, True, True, 0),
+                functools.partial(attention_backward_body, sizes, inner, layer, True, True, False),
                 blocks,
                 ins + others,
                 specs_from(0) + [rows_of(lanes)] + [fixed(weights_shape.shape)] * len(others),
@@ -1406,41 +1499,39 @@
                 2 * layers + 2 + 2 * layer,
             )
         else:
-            start = early * block if ships and early < blocks else 0
-            cut = (blocks + 1) // 2 if start else 0
+            cut = (blocks + 1) // 2 if ships else 0
             carried = ()
-            if start:
-                grad_state, attention_weights, sums, late_rows = call(
+            if ships:
+                grad_state, attention_weights, sums, head_rows = call(
                     functools.partial(
-                        attention_backward_body, sizes, inner, False, True, False, start
+                        attention_backward_body, sizes, inner, layer, True, False, True
                     ),
                     cut,
-                    ins + (columns, flat),
-                    specs_from(0) + [blocked(state), fixed(columns.shape), ANY],
-                    (wide_f32, weights_shape, back_shape, late_shape),
+                    ins + (columns, partial),
+                    specs_from(0)
+                    + [blocked(state), fixed(columns.shape), fixed(partial.shape)],
+                    (wide_f32, weights_shape, back_shape, rows_shape),
                     (
                         blocked(wide_f32),
                         fixed(weights_shape.shape),
                         fixed(back_shape.shape),
-                        ANY,
+                        fixed(rows_shape.shape),
                     ),
-                    scratch + SUM_SCRATCH + swap + row_sems,
+                    scratch
+                    + SUM_SCRATCH
+                    + sum_swap
+                    + [pltpu.VMEM(rows_shape.shape, BF16)]
+                    + row_sems,
                     25 * 10**9,
                     4 * layers + 1,
                 )
-                carried = (grad_state, attention_weights, sums)
-                parts = (early_rows, late_rows)
-            elif ships:
-                parts = (early_rows,)
-            if ships:
-                head_rows = head_gradient(sizes, inner, parts, batch_cotangent)
                 (*carried, grad_normed), head_rows = lax.optimization_barrier(
-                    ((*carried, grad_normed), head_rows)
+                    ((grad_state, attention_weights, sums, grad_normed), head_rows)
                 )
                 head_rows = spread_head(sizes, inner, head_rows)
             grad_state, attention_weights, back_two, rows_two = call(
                 functools.partial(
-                    attention_backward_body, sizes, inner, False, not carried, True, 0
+                    attention_backward_body, sizes, inner, layer, not carried, True, False
                 ),
                 blocks - cut,
                 (grad_normed,) + ins[1:] + (columns, *carried),
@@ -1458,7 +1549,7 @@
                     fixed(back_shape.shape),
                     fixed(tile_shape.shape),
                 ),
-                scratch + SUM_SCRATCH + swap,
+                scratch + SUM_SCRATCH + sum_swap,
                 25 * 10**9,
                 2 * layers + 2 + 2 * layer,
                 {len(ins) + 1: 0} if carried else None,

time: 368 us -> 334 us (0.908)
  Pallas kernels: 346 us -> 313 us
    pallas_call x12 -> x11, Pallas kernels: 346 us -> 307 us  [call(): pl.pallas_call(body, grid=(blocks,), in_specs=in_specs, out_specs=out_spe...]
    pallas_call x0 -> x1, Pallas kernels: none -> 6.54 us  [head_gradient(): pl.pallas_call(head_gradient_body, grid_spec=pltpu.PrefetchScalarGridSpec...]
  transfers between devices with their start and end apart: 2 -> 2, of which waited for: 1 -> 0; matrix products, arithmetic and copies ran while one was open for 1% -> 1% of each run, Pallas kernels for 90% -> 82%
where the time goes in v2:
time: 334 us; the launch traced here: 333 us
  Pallas kernels  313 us (94%)
  between operations  14.2 us (4%)
    pallas_call x11, Pallas kernels, call(): pl.pallas_call(body, grid=(blocks,), in_specs=in_specs, out_specs=out_spe...  307 us
  transfers between devices with their start and end apart: 2, of which 0 were waited for; matrix products, arithmetic and copies ran while one was open for 1% of the time, Pallas kernels for 82%

profile of v2, /device:TPU:0, one launch (start us, length us, event | category | flops | bytes accessed | tf_op | source)
XLA Modules:
  0.0 332.7 jit_solution(15191483142922441473)
XLA Ops:
  7.2 0.0 all-gather.5.cloned.1.call-start
  7.2 0.7 all-gather.5.cloned.1.call-update
  7.9 0.0 all-gather.7.cloned.1.call-start
  8.0 0.7 add_subtract_fusion
  8.7 0.9 fusion.1
  9.5 0.1 copy.22
  9.6 0.7 reshape.47.refs_4_.valid_ref.refs_8_.refs_5_
  10.3 34.0 %shard_map.178 = (f32[9,128,1024]{2,1,0:T(8,128)}, bf16[9,384,1024]{2,1,0:T(8,128)(2,1)}, bf16[9,128,1024]{2,1,0:T(8,128)(2,1)}, f32[9,16,1024]{2,1,0:T(8,128)},...) custom-call(bf16[9216,128]{1,0:T(8,128)(2,1)} %bitcast.14, bf16[720,4096]{1,0:T(8,128)(2,1)} %bitcast.11, ...), custom_call_target="tpu_custom_call" | custom-call | flops 20000000000 | bytes 29597696 | tf_op jit(solution)/shard_map/pallas_call | solution.py:1091
  44.3 18.2 %shard_map.179 = (f32[9,128,1024]{2,1,0:T(8,128)}, f32[6,128,128]{2,1,0:T(8,128)}) custom-call(f32[9,128,1024]{2,1,0:T(8,128)} %get-tuple-element.64.h_ref.refs_2_.refs_1_, f32[6,128,128]{2,1,0:T(8,128)} %get-tuple-element.65.columns.refs_5_.refs_6_, bf16[2,128,256]{2,1,0:T(8,128)(2,1)} %refs_7_.5, bf16[2,256,128]{2,1,0:T(8,128)(2,1)} %refs_6_.7, ...), custom_call_target="tpu_custom_call" | custom-call | flops 10000000000 | bytes 10526720 | tf_op jit(solution)/shard_map/pallas_call | solution.py:1091
  62.6 34.7 %shard_map.180 = (f32[9,128,1024]{2,1,0:T(8,128)}, bf16[9,384,1024]{2,1,0:T(8,128)(2,1)}, bf16[9,128,1024]{2,1,0:T(8,128)(2,1)}, f32[9,16,1024]{2,1,0:T(8,128)},...) custom-call(f32[9,128,1024]{2,1,0:T(8,128)} %get-tuple-element.66.refs_0_.refs_10_.refs_1_, ...), custom_call_target="tpu_custom_call" | custom-call | flops 20000000000 | bytes 37276160 | tf_op jit(solution)/shard_map/pallas_call | solution.py:1091
  97.3 18.3 %shard_map.181 = (f32[9,128,1024]{2,1,0:T(8,128)}, f32[6,128,128]{2,1,0:T(8,128)}) custom-call(f32[9,128,1024]{2,1,0:T(8,128)} %get-tuple-element.69.h_ref.refs_2_.refs_1_, f32[6,128,128]{2,1,0:T(8,128)} %get-tuple-element.70.columns.refs_5_.refs_6_, bf16[2,128,256]{2,1,0:T(8,128)(2,1)} %refs_7_.5, bf16[2,256,128]{2,1,0:T(8,128)(2,1)} %refs_6_.7, ...), custom_call_target="tpu_custom_call" | custom-call | flops 10000000000 | bytes 10526720 | tf_op jit(solution)/shard_map/pallas_call | solution.py:1091
  115.6 23.6 %shard_map.182 = (bf16[64,144,128]{2,1,0:T(8,128)(2,1)}, f32[9,128,1024]{2,1,0:T(8,128)}, f32[2,128,128]{2,1,0:T(8,128)}, f32[2,128]{1,0:T(2,128)}, bf16[16,4,64,128]{3,2,1,0:T(8,128)(2,1)}) custom-call(f32[9,128,1024]{2,1,0:T(8,128)} %get-tuple-element.71.f_ref.refs_1_, f32[6,128,128]{2,1,0:T(8,128)} %get-tuple-element.72.columns.refs_3_, ...), custom_call_target="tpu_custom_call" | custom-call | flops 1000000000 | bytes 18125824 | tf_op jit(solution)/shard_map/pallas_call | solution.py:1091
  139.1 31.0 %shard_map.183 = (f32[9,128,1024]{2,1,0:T(8,128)}, f32[512,128]{1,0:T(8,128)}, f32[2,128,128]{2,1,0:T(8,128)}, f32[2,128]{1,0:T(2,128)}, bf16[144,720]{1,0:T(8,128)(2,1)}, /*index=5*/bf16[16,4,80,128]{3,2,1,0:T(8,128)(2,1)}) custom-call(f32[9,128,1024]{2,1,0:T(8,128)} %get-tuple-element.74.refs_0_, f32[9,128,1024]{2,1,0:T(8,128)} %get-tuple-element.71.f_ref.refs_1_, ...), custom_call_target="tpu_custom_call" | custom-call | flops 20000000000 | bytes 38518272 | tf_op jit(solution)/shard_map/pallas_call | solution.py:1091
  170.2 0.0 all-gather.5.cloned.1.call-done
  170.2 6.5 %shard_map.184.refs_12_ = bf16[2,720,256]{2,1,0:T(8,128)(2,1)} custom-call(s32[1]{0:T(128)} %bitcast.2.half, bf16[16,4,64,128]{3,2,1,0:T(8,128)(2,1)} %get-tuple-element.79.refs_0_, bf16[16,4,80,128]{3,2,1,0:T(8,128)(2,1)} %get-tuple-element.80.refs_1_, bf16[32,144,720]{2,1,0:T(8,128)(2,1)} %bitcast.7), custom_call_target="tpu_custom_call" | custom-call | flops 1698693120 | bytes 5677056 | tf_op jit(solution)/shard_map/pallas_call | solution.py:1147
  176.7 26.7 %shard_map.185 = (f32[9,128,1024]{2,1,0:T(8,128)}, f32[512,128]{1,0:T(8,128)}, f32[2,128,128]{2,1,0:T(8,128)}, bf16[720,256]{1,0:T(8,128)(2,1)}) custom-call(f32[9,128,1024]{2,1,0:T(8,128)} %get-tuple-element.91.refs_0_, f32[9,128,1024]{2,1,0:T(8,128)} %get-tuple-element.69.h_ref.refs_2_.refs_1_, bf16[9,384,1024]{2,1,0:T(8,128)(2,1)} %get-tuple-element.82.refs_2_, ...), custom_call_target="tpu_custom_call" | custom-call | flops 24999999488 | bytes 31617024 | tf_op jit(solution)/shard_map/pallas_call | solution.py:1091
  203.4 0.0 all-gather.7.cloned.1.call-update
  203.4 27.4 %shard_map.186 = (f32[9,128,1024]{2,1,0:T(8,128)}, f32[512,128]{1,0:T(8,128)}, f32[2,128,128]{2,1,0:T(8,128)}, f32[2,128]{1,0:T(2,128)}) custom-call(f32[9,128,1024]{2,1,0:T(8,128)} %get-tuple-element.91.refs_0_, f32[9,128,1024]{2,1,0:T(8,128)} %get-tuple-element.69.h_ref.refs_2_.refs_1_, ...), custom_call_target="tpu_custom_call", output_to_operand_aliasing={{0}: (12, {})} | custom-call | flops 24999999488 | bytes 35623936 | tf_op jit(solution)/shard_map/pallas_call | solution.py:1091
  230.8 22.4 %shard_map.187 = (f32[9,128,1024]{2,1,0:T(8,128)}, f32[512,128]{1,0:T(8,128)}, f32[2,128,128]{2,1,0:T(8,128)}, f32[2,128]{1,0:T(2,128)}) custom-call(f32[9,128,1024]{2,1,0:T(8,128)} %get-tuple-element.95.refs_0_, f32[9,128,1024]{2,1,0:T(8,128)} %get-tuple-element.66.refs_0_.refs_10_.refs_1_, f32[9,128,1024]{2,1,0:T(8,128)} %get-tuple-element.64.h_ref.refs_2_.refs_1_, ...), custom_call_target="tpu_custom_call" | custom-call | flops 20000000000 | bytes 20485120 | tf_op jit(solution)/shard_map/pallas_call | solution.py:1091
  253.2 62.2 %shard_map.188 = (bf16[9216,128]{1,0:T(8,128)(2,1)}, bf16[4,512,128]{2,1,0:T(8,128)(2,1)}) custom-call(f32[9,128,1024]{2,1,0:T(8,128)} %get-tuple-element.97.refs_0_, f32[9,128,1024]{2,1,0:T(8,128)} %get-tuple-element.64.h_ref.refs_2_.refs_1_, bf16[9,384,1024]{2,1,0:T(8,128)(2,1)} %get-tuple-element.98.refs_2_, ...), custom_call_target="tpu_custom_call" | custom-call | flops 49999998976 | bytes 26316800 | tf_op jit(solution)/shard_map/pallas_call | solution.py:1091
  315.4 0.0 copy-start.1
  315.4 0.0 copy-start
  315.5 0.0 all-gather.7.cloned.1.call-done
  315.5 8.3 %shard_map.189 = (f32[720,4096]{1,0:T(8,128)}, f32[2,3,128,128]{3,2,1,0:T(8,128)}, f32[2,128,128]{2,1,0:T(8,128)}, f32[2,128,256]{2,1,0:T(8,128)}, f32[2,256,128...) custom-call(bf16[2,8,720,256]{3,2,1,0:T(8,128)(2,1)} %bitcast.8, ...), custom_call_target="tpu_custom_call" | custom-call | flops 1 | bytes 19275776 | tf_op jit(solution)/shard_map/pallas_call | solution.py:1091
  323.8 0.0 copy-done.1
  323.8 0.7 copy.36
  324.5 0.0 copy-done
  324.5 1.4 copy.37
Async XLA Ops:
  7.2 163.0 %all-gather.5.cloned.1.call-start = ((), (), s32[]{:S(2)}) async-start(), calls=%async_computation | async-start | bytes 7299072 | tf_op jit(solution)/shard_map/all_gather | solution.py:1259
  7.9 307.6 %all-gather.7.cloned.1.call-start = ((), (), s32[]{:S(2)}) async-start(), calls=%async_computation.1 | async-start | bytes 6266880 | tf_op jit(solution)/shard_map/all_gather | solution.py:1177
  315.4 8.3 %copy-start.1 = (bf16[144,720]{1,0:T(8,128)(2,1)S(1)}, bf16[144,720]{1,0:T(8,128)(2,1)}, u32[]{:S(2)}) copy-start(bf16[144,720]{1,0:T(8,128)(2,1)} %get-tuple-element.128) | copy-start | bytes 622084
  315.4 9.0 %copy-start = (bf16[9216,128]{1,0:T(8,128)(2,1)S(1)}, bf16[9216,128]{1,0:T(8,128)(2,1)}, u32[]{:S(2)}) copy-start(bf16[9216,128]{1,0:T(8,128)(2,1)} %get-tuple-element.105) | copy-start | bytes 7077892
Sparse Core Ops, SparseCore 0:
  10.9 75.1 all-gather.4
  203.6 107.3 all-gather.6

commit v3 on v2

--- a/solution.py
+++ b/solution.py
@@ -143,6 +143,18 @@
         work(slice(start, start + CHUNK))
 
 
+def each(count, work):
+    if count == 1:
+        work(0)
+        return
+
+    def one(index, carry):
+        work(index)
+        return carry
+
+    lax.fori_loop(0, count, one, 0)
+
+
 def device_at(index, sizes):
     return index // sizes[1], lax.rem(index, sizes[1])
 
@@ -172,7 +184,7 @@
     return jnp.minimum(1, pl.num_programs(0) - 1)
 
 
-def swap_tiles(sizes, tiles, send, arrive):
+def swap_tiles(sizes, tiles, send, arrive, meanwhile=None):
     others = sizes[0] * sizes[1]
     own = lax.axis_index("dp") * sizes[1] + lax.axis_index("patch")
 
@@ -188,6 +200,8 @@
         return carry
 
     lax.fori_loop(1, others, start, 0)
+    if meanwhile is not None:
+        meanwhile()
     await_bytes(tiles.at[pl.ds(0, others - 1)], arrive)
     await_bytes(tiles.at[pl.ds(0, others - 1)], send)
 
@@ -335,18 +349,30 @@
     )
 
 
-def partner_copy(sizes, inner, partial, got, sems):
-    chip = lax.axis_index("dp")
-    half = lax.rem(chip, inner) // (inner // 2)
-    other = chip + (1 - 2 * half) * (inner // 2)
-    return half, pltpu.make_async_remote_copy(
-        src_ref=partial.at[1 - half],
-        dst_ref=got,
-        send_sem=sems.at[0],
-        recv_sem=sems.at[1],
-        device_id=(other, lax.axis_index("patch")),
-        device_id_type=pl.DeviceIdType.MESH,
-    )
+class Partner:
+    def __init__(self, sizes, inner, partial, got, sems):
+        chip = lax.axis_index("dp")
+        self.half = lax.rem(chip, inner) // (inner // 2)
+        self.other = chip + (1 - 2 * self.half) * (inner // 2)
+        self.partial, self.got, self.sems = partial, got, sems
+
+    def start(self):
+        rows = self.got.shape[0]
+        runs = math.gcd(rows // 16, 3) if rows % 16 == 0 else 1
+        for run in range(runs):
+            part = pl.ds(run * (rows // runs), rows // runs)
+            pltpu.make_async_remote_copy(
+                src_ref=self.partial.at[1 - self.half, part],
+                dst_ref=self.got.at[part],
+                send_sem=self.sems.at[0],
+                recv_sem=self.sems.at[1],
+                device_id=(self.other, lax.axis_index("patch")),
+                device_id_type=pl.DeviceIdType.MESH,
+            ).start()
+
+    def wait(self):
+        await_bytes(self.got, self.sems.at[1])
+        await_bytes(self.got, self.sems.at[0])
 
 
 def as_columns(row):
@@ -359,20 +385,20 @@
 
     @pl.when(step == 0)
     def _():
-        own = jnp.sum(valid[...])
-        first = jnp.sum(fold_lanes(values[...] * valid[...]), axis=1, keepdims=True) / own
+        own = jnp.sum(valid[0])
+        first = jnp.sum(fold_lanes(values[0] * valid[0]), axis=1, keepdims=True) / own
         pivot[...] = jnp.broadcast_to(first, (WIDTH, WIDTH))
         sums[...] = jnp.zeros_like(sums)
         squares[...] = jnp.zeros_like(squares)
         count[...] = jnp.zeros_like(count)
 
-    def add(at):
-        centred = (values[:, at] - wide(pivot[...], CHUNK)) * valid[:, at]
+    def add(index, at):
+        centred = (values[index, :, at] - wide(pivot[...], CHUNK)) * valid[index, :, at]
         sums[...] += fold_lanes(centred)
         squares[...] += fold_lanes(centred * centred)
-        count[...] += jnp.broadcast_to(fold_lanes(valid[:, at]), count.shape)
-
-    chunks(lanes, add)
+        count[...] += jnp.broadcast_to(fold_lanes(valid[index, :, at]), count.shape)
+
+    each(values.shape[0], lambda index: chunks(lanes, functools.partial(add, index)))
 
     @pl.when(step == pl.num_programs(0) - 1)
     def _():
@@ -384,7 +410,12 @@
         tiles[own, 1:2, :] = square - shift * shift / total
         tiles[own, 2:3, :] = total
         tiles[own, 3:4, :] = total
-        swap_tiles(sizes, tiles, send, arrive)
+
+        def known():
+            out[3] = as_columns(gains[1])
+            out[5] = as_columns(gains[0])
+
+        swap_tiles(sizes, tiles, send, arrive, known)
         means, spreads, counts = tiles[:, 0, :], tiles[:, 1, :], tiles[:, 2, :]
         total = jnp.sum(counts, axis=0, keepdims=True)
         mean = jnp.sum(means * counts, axis=0, keepdims=True) / total
@@ -394,9 +425,7 @@
         out[0] = as_columns(mean)
         out[1] = as_columns(inverse)
         out[2] = as_columns(inverse * gains[0])
-        out[3] = as_columns(gains[1])
         out[4] = as_columns(total)
-        out[5] = as_columns(gains[0])
 
 
 def add_gradient(grad, normal, valid, scratch):
@@ -563,7 +592,7 @@
             readout_copy(readout, readout_out, readout_sems).wait()
 
     gains = scales[layer, 0:1, :], offsets[layer, 0:1, :]
-    norm_stats(step, sizes, h_out.at[0], valid_ref.at[0], gains, columns_out, scratch)
+    norm_stats(step, sizes, h_out, valid_ref, gains, columns_out, scratch)
 
 
 def feed_forward_body(
@@ -583,20 +612,17 @@
         w_up[...] = turn(w_up_ref[0])
         w_down[...] = turn(w_down_ref[0])
 
-    def feed(at):
-        normed = apply_norm(h_ref[0, :, at], columns)
-        low = normed.astype(BF16)
-        active = []
-        for start in range(0, w_up.shape[0], WIDTH):
-            u = dot(w_up[start : start + WIDTH, :], low).astype(BF16).astype(F32)
-            bent = jnp.tanh(u * (GELU_IN + (GELU_IN * GELU_CUBE) * (u * u)))
-            half = 0.5 * u
-            active.append((half + half * bent).astype(BF16))
-        f_out[0, :, at] = normed + dot(w_down[...], jnp.concatenate(active, axis=0))
-
-    chunks(h_ref.shape[-1], feed)
+    def feed(index, at):
+        normed = apply_norm(h_ref[index, :, at], columns)
+        u = dot(w_up[...], normed.astype(BF16)).astype(BF16).astype(F32)
+        bent = jnp.tanh(u * (GELU_IN + (GELU_IN * GELU_CUBE) * (u * u)))
+        half = 0.5 * u
+        active = (half + half * bent).astype(BF16)
+        f_out[index, :, at] = normed + dot(w_down[...], active)
+
+    each(h_ref.shape[0], lambda index: chunks(h_ref.shape[-1], functools.partial(feed, index)))
     gains = scales[layer, 1:2, :], offsets[layer, 1:2, :]
-    norm_stats(step, sizes, f_out.at[0], valid_ref.at[0], gains, columns_out, scratch)
+    norm_stats(step, sizes, f_out, valid_ref, gains, columns_out, scratch)
 
 
 def turn_body(
@@ -871,7 +897,7 @@
             gx_out, weights_out, made, *refs = refs
         if start:
             rows_out, *refs, got, row_sems = refs
-            half, partner = partner_copy(sizes, inner, partial, got, row_sems)
+            partner = Partner(sizes, inner, partial, got, row_sems)
         count = len(SUM_SCRATCH) + len(swap_scratch(sizes, 2))
         refs, scratch = refs[:-count], refs[-count:]
     size = len(BACKWARD_SLOT)
@@ -1011,10 +1037,20 @@
 
     pipeline(pairs, slots, score, soften, mix)
 
+    def add_weights():
+        for part in range(3):
+            rows = slice(part * WIDTH, (part + 1) * WIDTH)
+            weights_out[(part + 1) * WIDTH : (part + 2) * WIDTH, :] += dot_rows(
+                low_full[...], grads[rows, :]
+            )
+
+    if first_layer:
+        low_full[...] = x_ref[...].astype(F32).T.astype(BF16)
+        add_weights()
+        pl.when(step == last)(shares[0].begin)
+
     def finish(at):
-        if first_layer:
-            low_full[:, at] = x_ref[at, :].astype(F32).T.astype(BF16)
-        else:
+        if not first_layer:
             normal = normalise(x_ref[0, :, at], columns_prev)
             inputs = normal * wide(columns_prev[5], CHUNK) + wide(columns_prev[3], CHUNK)
             low_full[:, at] = inputs.astype(BF16)
@@ -1026,16 +1062,12 @@
             add_gradient(grad, normal, valid_ref[0, :, at], scratch)
 
     chunks(lanes, finish)
-    for part in range(3):
-        rows = slice(part * WIDTH, (part + 1) * WIDTH)
-        weights_out[(part + 1) * WIDTH : (part + 2) * WIDTH, :] += dot_rows(
-            low_full[...], grads[rows, :]
-        )
+    if not first_layer:
+        add_weights()
     if first_layer:
 
         @pl.when(step == last)
         def _():
-            shares[0].begin()
             for share in shares[1:]:
                 share.stages[0].drain()
                 share.stages[1].finish()
@@ -1051,7 +1083,7 @@
             @pl.when(step == last)
             def _():
                 partner.wait()
-                total = partial[half].astype(F32) + got[...].astype(F32)
+                total = partial[partner.half].astype(F32) + got[...].astype(F32)
                 rows_out[...] = total.astype(rows_out.dtype)
 
         if closes:
@@ -1070,6 +1102,10 @@
 
 def blocked(array, first=0):
     return pl.BlockSpec((1,) + array.shape[1:], lambda step: (first + step, 0, 0))
+
+
+def grouped(array, group):
+    return pl.BlockSpec((group,) + array.shape[1:], lambda step: (step, 0, 0))
 
 
 def rows_of(lanes):
@@ -1250,6 +1286,7 @@
     flat_spec, own_spec, other_spec = head_specs(horizon, half_rows, patches, series)
     pm_f32 = shaped((patches, series, width))
     pm_bf16 = shaped((patches, series, width), BF16)
+    group = 3 if blocks % 3 == 0 else 1
     series_spec = pl.BlockSpec((patches, block, width), lambda step: (0, step, 0))
     weights_shape = shaped((4 * width, width))
     stat_swap, sum_swap = swap_scratch(sizes, 4), swap_scratch(sizes, 2)
@@ -1318,7 +1355,7 @@
             (grad_rows,) = extra
         summed, columns_two = call(
             functools.partial(feed_forward_body, sizes, layer),
-            blocks,
+            blocks // group,
             (
                 attended,
                 columns_one,
@@ -1329,15 +1366,15 @@
                 batchnorm_offsets,
             ),
             [
-                blocked(attended),
+                grouped(attended, group),
                 fixed(columns_one.shape),
                 fixed(first_dense_matrices.shape),
                 fixed(second_dense_matrices.shape),
-                blocked(valid_rows),
+                grouped(valid_rows, group),
             ]
             + norm_specs,
             (wide_f32, columns_shape),
-            (blocked(wide_f32), fixed(columns_shape.shape)),
+            (grouped(wide_f32, group), fixed(columns_shape.shape)),
             [pltpu.VMEM((hidden, width), BF16), pltpu.VMEM((width, hidden), BF16)]
             + STAT_SCRATCH
             + stat_swap,

time: 334 us -> 331 us (level)
  no operation moved by 1% of the time
where the time goes in v3:
time: 331 us; the launch traced here: 330 us
  Pallas kernels  310 us (94%)
  between operations  14.2 us (4%)
    pallas_call x11, Pallas kernels, call(): pl.pallas_call(body, grid=(blocks,), in_specs=in_specs, out_specs=out_spe...  304 us
  transfers between devices with their start and end apart: 2, of which 0 were waited for; matrix products, arithmetic and copies ran while one was open for 1% of the time, Pallas kernels for 82%

profile of v3, /device:TPU:0, one launch (start us, length us, event | category | flops | bytes accessed | tf_op | source)
XLA Modules:
  0.0 329.9 jit_solution(14196781012562311233)
XLA Ops:
  7.2 0.0 all-gather.5.cloned.1.call-start
  7.2 0.7 all-gather.5.cloned.1.call-update
  7.9 0.0 all-gather.7.cloned.1.call-start
  8.0 0.7 add_subtract_fusion
  8.7 0.9 fusion.1
  9.5 0.1 copy.22
  9.6 0.7 reshape.47.refs_4_.valid_ref.refs_8_.refs_5_
  10.3 34.0 %shard_map.178 = (f32[9,128,1024]{2,1,0:T(8,128)}, bf16[9,384,1024]{2,1,0:T(8,128)(2,1)}, bf16[9,128,1024]{2,1,0:T(8,128)(2,1)}, f32[9,16,1024]{2,1,0:T(8,128)},...) custom-call(bf16[9216,128]{1,0:T(8,128)(2,1)} %bitcast.14, bf16[720,4096]{1,0:T(8,128)(2,1)} %bitcast.11, ...), custom_call_target="tpu_custom_call" | custom-call | flops 20000000000 | bytes 29597696 | tf_op jit(solution)/shard_map/pallas_call | solution.py:1127
  44.3 16.5 %shard_map.179 = (f32[9,128,1024]{2,1,0:T(8,128)}, f32[6,128,128]{2,1,0:T(8,128)}) custom-call(f32[9,128,1024]{2,1,0:T(8,128)} %get-tuple-element.64.h_ref.refs_2_.refs_1_, f32[6,128,128]{2,1,0:T(8,128)} %get-tuple-element.65.columns.refs_5_.refs_6_, bf16[2,128,256]{2,1,0:T(8,128)(2,1)} %refs_7_.5, bf16[2,256,128]{2,1,0:T(8,128)(2,1)} %refs_6_.7, ...), custom_call_target="tpu_custom_call" | custom-call | flops 10000000000 | bytes 10526720 | tf_op jit(solution)/shard_map/pallas_call | solution.py:1127
  60.8 34.7 %shard_map.180 = (f32[9,128,1024]{2,1,0:T(8,128)}, bf16[9,384,1024]{2,1,0:T(8,128)(2,1)}, bf16[9,128,1024]{2,1,0:T(8,128)(2,1)}, f32[9,16,1024]{2,1,0:T(8,128)},...) custom-call(f32[9,128,1024]{2,1,0:T(8,128)} %get-tuple-element.66.refs_0_.refs_10_.refs_1_, ...), custom_call_target="tpu_custom_call" | custom-call | flops 20000000000 | bytes 37276160 | tf_op jit(solution)/shard_map/pallas_call | solution.py:1127
  95.5 15.9 %shard_map.181 = (f32[9,128,1024]{2,1,0:T(8,128)}, f32[6,128,128]{2,1,0:T(8,128)}) custom-call(f32[9,128,1024]{2,1,0:T(8,128)} %get-tuple-element.69.h_ref.refs_2_.refs_1_, f32[6,128,128]{2,1,0:T(8,128)} %get-tuple-element.70.columns.refs_5_.refs_6_, bf16[2,128,256]{2,1,0:T(8,128)(2,1)} %refs_7_.5, bf16[2,256,128]{2,1,0:T(8,128)(2,1)} %refs_6_.7, ...), custom_call_target="tpu_custom_call" | custom-call | flops 10000000000 | bytes 10526720 | tf_op jit(solution)/shard_map/pallas_call | solution.py:1127
  111.5 24.0 %shard_map.182 = (bf16[64,144,128]{2,1,0:T(8,128)(2,1)}, f32[9,128,1024]{2,1,0:T(8,128)}, f32[2,128,128]{2,1,0:T(8,128)}, f32[2,128]{1,0:T(2,128)}, bf16[16,4,64,128]{3,2,1,0:T(8,128)(2,1)}) custom-call(f32[9,128,1024]{2,1,0:T(8,128)} %get-tuple-element.71.f_ref.refs_1_, f32[6,128,128]{2,1,0:T(8,128)} %get-tuple-element.72.columns.refs_3_, ...), custom_call_target="tpu_custom_call" | custom-call | flops 1000000000 | bytes 18125824 | tf_op jit(solution)/shard_map/pallas_call | solution.py:1127
  135.5 31.1 %shard_map.183 = (f32[9,128,1024]{2,1,0:T(8,128)}, f32[512,128]{1,0:T(8,128)}, f32[2,128,128]{2,1,0:T(8,128)}, f32[2,128]{1,0:T(2,128)}, bf16[144,720]{1,0:T(8,128)(2,1)}, /*index=5*/bf16[16,4,80,128]{3,2,1,0:T(8,128)(2,1)}) custom-call(f32[9,128,1024]{2,1,0:T(8,128)} %get-tuple-element.74.refs_0_, f32[9,128,1024]{2,1,0:T(8,128)} %get-tuple-element.71.f_ref.refs_1_, ...), custom_call_target="tpu_custom_call" | custom-call | flops 20000000000 | bytes 38518272 | tf_op jit(solution)/shard_map/pallas_call | solution.py:1127
  166.5 0.0 all-gather.5.cloned.1.call-done
  166.6 6.5 %shard_map.184.refs_12_ = bf16[2,720,256]{2,1,0:T(8,128)(2,1)} custom-call(s32[1]{0:T(128)} %bitcast.2.half, bf16[16,4,64,128]{3,2,1,0:T(8,128)(2,1)} %get-tuple-element.79.refs_0_, bf16[16,4,80,128]{3,2,1,0:T(8,128)(2,1)} %get-tuple-element.80.refs_1_, bf16[32,144,720]{2,1,0:T(8,128)(2,1)} %bitcast.7), custom_call_target="tpu_custom_call" | custom-call | flops 1698693120 | bytes 5677056 | tf_op jit(solution)/shard_map/pallas_call | solution.py:1183
  173.1 26.7 %shard_map.185 = (f32[9,128,1024]{2,1,0:T(8,128)}, f32[512,128]{1,0:T(8,128)}, f32[2,128,128]{2,1,0:T(8,128)}, bf16[720,256]{1,0:T(8,128)(2,1)}) custom-call(f32[9,128,1024]{2,1,0:T(8,128)} %get-tuple-element.91.refs_0_, f32[9,128,1024]{2,1,0:T(8,128)} %get-tuple-element.69.h_ref.refs_2_.refs_1_, bf16[9,384,1024]{2,1,0:T(8,128)(2,1)} %get-tuple-element.82.refs_2_, ...), custom_call_target="tpu_custom_call" | custom-call | flops 24999999488 | bytes 31617024 | tf_op jit(solution)/shard_map/pallas_call | solution.py:1127
  199.8 0.0 all-gather.7.cloned.1.call-update
  199.9 27.3 %shard_map.186 = (f32[9,128,1024]{2,1,0:T(8,128)}, f32[512,128]{1,0:T(8,128)}, f32[2,128,128]{2,1,0:T(8,128)}, f32[2,128]{1,0:T(2,128)}) custom-call(f32[9,128,1024]{2,1,0:T(8,128)} %get-tuple-element.91.refs_0_, f32[9,128,1024]{2,1,0:T(8,128)} %get-tuple-element.69.h_ref.refs_2_.refs_1_, ...), custom_call_target="tpu_custom_call", output_to_operand_aliasing={{0}: (12, {})} | custom-call | flops 24999999488 | bytes 35623936 | tf_op jit(solution)/shard_map/pallas_call | solution.py:1127
  227.2 22.4 %shard_map.187 = (f32[9,128,1024]{2,1,0:T(8,128)}, f32[512,128]{1,0:T(8,128)}, f32[2,128,128]{2,1,0:T(8,128)}, f32[2,128]{1,0:T(2,128)}) custom-call(f32[9,128,1024]{2,1,0:T(8,128)} %get-tuple-element.95.refs_0_, f32[9,128,1024]{2,1,0:T(8,128)} %get-tuple-element.66.refs_0_.refs_10_.refs_1_, f32[9,128,1024]{2,1,0:T(8,128)} %get-tuple-element.64.h_ref.refs_2_.refs_1_, ...), custom_call_target="tpu_custom_call" | custom-call | flops 20000000000 | bytes 20485120 | tf_op jit(solution)/shard_map/pallas_call | solution.py:1127
  249.6 62.9 %shard_map.188 = (bf16[9216,128]{1,0:T(8,128)(2,1)}, bf16[4,512,128]{2,1,0:T(8,128)(2,1)}) custom-call(f32[9,128,1024]{2,1,0:T(8,128)} %get-tuple-element.97.refs_0_, f32[9,128,1024]{2,1,0:T(8,128)} %get-tuple-element.64.h_ref.refs_2_.refs_1_, bf16[9,384,1024]{2,1,0:T(8,128)(2,1)} %get-tuple-element.98.refs_2_, ...), custom_call_target="tpu_custom_call" | custom-call | flops 49999998976 | bytes 26316800 | tf_op jit(solution)/shard_map/pallas_call | solution.py:1127
  312.6 0.0 copy-start.1
  312.6 0.0 copy-start
  312.6 0.0 all-gather.7.cloned.1.call-done
  312.6 8.3 %shard_map.189 = (f32[720,4096]{1,0:T(8,128)}, f32[2,3,128,128]{3,2,1,0:T(8,128)}, f32[2,128,128]{2,1,0:T(8,128)}, f32[2,128,256]{2,1,0:T(8,128)}, f32[2,256,128...) custom-call(bf16[2,8,720,256]{3,2,1,0:T(8,128)(2,1)} %bitcast.8, ...), custom_call_target="tpu_custom_call" | custom-call | flops 1 | bytes 19275776 | tf_op jit(solution)/shard_map/pallas_call | solution.py:1127
  320.9 0.0 copy-done.1
  320.9 0.7 copy.36
  321.6 0.0 copy-done
  321.6 1.4 copy.37
Async XLA Ops:
  7.2 159.4 %all-gather.5.cloned.1.call-start = ((), (), s32[]{:S(2)}) async-start(), calls=%async_computation | async-start | bytes 7299072 | tf_op jit(solution)/shard_map/all_gather | solution.py:1296
  7.9 304.7 %all-gather.7.cloned.1.call-start = ((), (), s32[]{:S(2)}) async-start(), calls=%async_computation.1 | async-start | bytes 6266880 | tf_op jit(solution)/shard_map/all_gather | solution.py:1213
  312.6 8.3 %copy-start.1 = (bf16[144,720]{1,0:T(8,128)(2,1)S(1)}, bf16[144,720]{1,0:T(8,128)(2,1)}, u32[]{:S(2)}) copy-start(bf16[144,720]{1,0:T(8,128)(2,1)} %get-tuple-element.128) | copy-start | bytes 622084
  312.6 9.0 %copy-start = (bf16[9216,128]{1,0:T(8,128)(2,1)S(1)}, bf16[9216,128]{1,0:T(8,128)(2,1)}, u32[]{:S(2)}) copy-start(bf16[9216,128]{1,0:T(8,128)(2,1)} %get-tuple-element.105) | copy-start | bytes 7077892
Sparse Core Ops, SparseCore 0:
  10.9 75.2 all-gather.4
  200.0 105.0 all-gather.6
